TPU v7x, 32 devices: a whole 2x2x4 slice. The times are simulated.
32 devices in a mesh: req: 8 (over z, y), mp: 4 (over x, core).
Axes of the slice: x: 2, y: 2, z: 4, core: 2. Of those that a mesh axis runs over, the one named last changes fastest.
Arguments:
- q_pre: bfloat16 [4096, 3072], P('req', 'mp'), may hold values from -64 to 64
- k_pre: bfloat16 [4096, 1024], P('req', 'mp'), may hold values from -64 to 64
- v_pre: bfloat16 [4096, 1024], P('req', 'mp'), may hold values from -12 to 12
- q_bias: float32 [3072], P('mp'), may hold values from -3 to 3
- k_bias: float32 [1024], P('mp'), may hold values from -3 to 3
- v_bias: float32 [1024], P('mp'), may hold values from -3 to 3
- segment_ids: int32 [4096], P('req'), may hold values from -1 to 31, as said below
- lengths: int32 [8, 4], replicated, may hold values from 64 to 128, as said below
- page_table: int32 [8, 4], replicated, may hold values from 0 to 31, as said below
- w_out: bfloat16 [3072, 5120], P('mp'), may hold values from -0.109375 to 0.109375
- residual: bfloat16 [4096, 5120], P('req'), may hold values from -4 to 4
- norm_gain: float32 [5120], replicated, may hold values from 0.1 to 1.9
- w_gate: bfloat16 [5120, 6912], P('req', 'mp'), may hold values from -0.078125 to 0.078125
- w_up: bfloat16 [5120, 6912], P('req', 'mp'), may hold values from -0.078125 to 0.078125
Outputs:
- hidden: bfloat16 [4096, 6912], P('req', 'mp')
- kv_cache: bfloat16 [32, 8, 128, 256], P('req', 'mp')
Inputs may be any that keep to these rules, and one draw needn't show every extreme that they name: Requests of block r lie in order from the block's first token, request j taking lengths[r, j] tokens; in every block one request has exactly 128 tokens. `segment_ids`: token t of block r carries r * 4 + j inside request j's run of tokens given by lengths, and -1 after the last request of its block. `page_table`: every page is named once; page p is held by req index p // 4; the requests of one block have pages held by different req indices.
All inputs are finite; a program needn't handle non-finite values.
Results may differ from a plain program's by a relative error of at most 0.019.
Values may be sent and summed in bfloat16 or wider, within the bound.
No kernel may reach another device: no remote copies, remote signals or barrier semaphores. Data moves between devices by JAX's collectives and lax.ppermute only.
A program may use at most 128 MiB of HBM per device.

v0:
```python
import math

import jax
import jax.numpy as jnp
from jax import lax
from jax.sharding import PartitionSpec as P

HD = 128
PAGE = 128
REQS = 4


THETA = 1000000.0
EPS = 1e-06


def rotate(values, positions):
    half_dim = values.shape[-1] // 2
    frequencies = THETA ** (-jnp.arange(half_dim, dtype=jnp.float32) * (2.0 / values.shape[-1]))
    angles = positions[:, None] * frequencies[None, :]
    cosine = jnp.cos(angles)[:, None, :]
    sine_part = jnp.sin(angles)[:, None, :]
    first_half = values[..., :half_dim]
    second = values[..., half_dim:]
    return jnp.concatenate(
        [first_half * cosine - second * sine_part, second * cosine + first_half * sine_part],
        axis=-1,
    )


def attend(queries, keys, values, length):
    scale_factor = 1.0 / math.sqrt(queries.shape[-1])
    scores = (
        jnp.einsum("sqhge,skhe->shgqk", queries, keys, preferred_element_type=jnp.float32)
        * scale_factor
    )
    page_len = queries.shape[1]
    query_pos = jnp.arange(page_len)[:, None]
    key_pos = jnp.arange(page_len)[None, :]
    allowed = (key_pos <= query_pos)[None] & (key_pos[None] < length[:, None, None])
    allowed = allowed[:, None, None]
    row_max = jnp.max(jnp.where(allowed, scores, -1e30), axis=-1, keepdims=True)
    weights = jnp.where(allowed, jnp.exp(scores - row_max), 0.0)
    row_sum = jnp.sum(weights, axis=-1, keepdims=True)
    present = (jnp.arange(page_len)[None, :] < length[:, None])[:, None, None, :, None]
    row_probs = jnp.where(present, weights / jnp.where(present, row_sum, 1.0), 0.0).astype(
        jnp.bfloat16
    )
    mixed_rows = jnp.einsum(
        "shgqk,skhe->sqhge", row_probs, values, preferred_element_type=jnp.float32
    )
    return mixed_rows.astype(jnp.bfloat16)


def normalize(resid_rows, summed, gain_row):
    state = resid_rows.astype(jnp.float32) + summed
    scale_row = lax.rsqrt(jnp.mean(state * state, axis=-1, keepdims=True) + EPS)
    return (state * scale_row * gain_row).astype(jnp.bfloat16)


def shards(
    q_pre,
    k_pre,
    v_pre,
    q_bias,
    k_bias,
    v_bias,
    segment_ids,
    lengths,
    page_table,
    w_out,
    residual,
    norm_gain,
    w_gate,
    w_up,
):
    me_req = lax.axis_index("req")
    groups_all = lax.axis_size("req")
    block_rows = q_pre.shape[0]
    kv_heads = k_pre.shape[1] // HD
    q_heads = q_pre.shape[1] // HD
    group_size = q_heads // kv_heads
    own_lens = lax.dynamic_index_in_dim(lengths, me_req, 0, keepdims=False)
    own_pages = lax.dynamic_index_in_dim(page_table, me_req, 0, keepdims=False)
    own_owner = own_pages // REQS
    starts = jnp.cumsum(own_lens) - own_lens
    offsets = jnp.arange(PAGE, dtype=jnp.int32)
    row_index = jnp.clip(starts[:, None] + offsets[None, :], 0, block_rows - 1)
    flat_index = row_index.reshape(-1)
    request_ids = me_req * REQS + jnp.arange(REQS, dtype=jnp.int32)[:, None]
    inside = (offsets[None, :] < own_lens[:, None]) & (
        jnp.take(segment_ids, flat_index).reshape(REQS, PAGE) == request_ids
    )
    keep_mask = inside[:, :, None, None]
    positions = offsets.astype(jnp.float32)

    def prepare(source, bias_row, head_count):
        picked = jnp.take(source, flat_index, axis=0).astype(jnp.float32) + bias_row
        return picked.reshape(REQS, PAGE, head_count, HD)

    query_req = jnp.where(
        keep_mask, rotate(prepare(q_pre, q_bias, q_heads), positions), 0.0
    ).astype(jnp.bfloat16)
    key_req = jnp.where(keep_mask, rotate(prepare(k_pre, k_bias, kv_heads), positions), 0.0).astype(
        jnp.bfloat16
    )
    value_req = jnp.where(keep_mask, prepare(v_pre, v_bias, kv_heads), 0.0).astype(jnp.bfloat16)
    to_owner = (own_owner[None, :] == jnp.arange(groups_all)[:, None]).astype(jnp.bfloat16)
    alive_rows = segment_ids >= 0
    req_idx = jnp.clip(segment_ids - me_req * REQS, 0, REQS - 1)
    req_hit = req_idx[:, None] == jnp.arange(REQS)[None, :]
    row_start = jnp.sum(jnp.where(req_hit, starts[None, :], 0), axis=1)
    row_pos = jnp.clip(jnp.arange(block_rows, dtype=jnp.int32) - row_start, 0, PAGE - 1)
    hits = (
        page_table[None, :, :] == (me_req * REQS + jnp.arange(REQS, dtype=jnp.int32))[:, None, None]
    )
    page_select = jnp.sum(hits.astype(jnp.int32), axis=2).astype(jnp.bfloat16)
    q_send = jnp.einsum(
        "gj,jpc->gpc",
        to_owner,
        query_req.reshape(REQS, PAGE, q_heads * HD),
        preferred_element_type=jnp.float32,
    ).astype(jnp.bfloat16)
    k_send = jnp.einsum(
        "gj,jpc->gpc",
        to_owner,
        key_req.reshape(REQS, PAGE, kv_heads * HD),
        preferred_element_type=jnp.float32,
    ).astype(jnp.bfloat16)
    v_send = jnp.einsum(
        "gj,jpc->gpc",
        to_owner,
        value_req.reshape(REQS, PAGE, kv_heads * HD),
        preferred_element_type=jnp.float32,
    ).astype(jnp.bfloat16)
    q_in, k_in, v_in = (
        lax.all_to_all(q_send, "req", split_axis=0, concat_axis=0, tiled=True),
        lax.all_to_all(k_send, "req", split_axis=0, concat_axis=0, tiled=True),
        lax.all_to_all(v_send, "req", split_axis=0, concat_axis=0, tiled=True),
    )
    in_len = jnp.sum(jnp.where(page_table // REQS == me_req, lengths, 0), axis=1)
    q_groups = q_in.reshape(groups_all, PAGE, kv_heads, group_size, HD)
    k_groups = k_in.reshape(groups_all, PAGE, kv_heads, HD)
    v_groups = v_in.reshape(groups_all, PAGE, kv_heads, HD)
    pages_in = jnp.concatenate([k_groups, v_groups], axis=-1).transpose(0, 2, 1, 3)
    attended = attend(q_groups, k_groups, v_groups, in_len)
    returned = lax.all_to_all(
        attended.reshape(groups_all, PAGE, q_heads * HD),
        "req",
        split_axis=0,
        concat_axis=0,
        tiled=True,
    )
    row_group = jnp.sum(jnp.where(req_hit, own_owner[None, :], 0), axis=1)
    source_rows = jnp.take(
        returned.reshape(groups_all * PAGE, q_heads * HD), row_group * PAGE + row_pos, axis=0
    )
    cache_out = jnp.einsum(
        "ls,shpc->lhpc", page_select, pages_in, preferred_element_type=jnp.float32
    ).astype(jnp.bfloat16)
    attn_rows = jnp.where(alive_rows[:, None], source_rows, jnp.zeros((), jnp.bfloat16))
    summed = lax.psum(
        jnp.dot(attn_rows, w_out, preferred_element_type=jnp.float32).astype(jnp.bfloat16), "mp"
    ).astype(jnp.float32)
    normed = normalize(residual, summed, norm_gain)
    gate_acc = jnp.dot(
        normed,
        lax.all_gather(w_gate, "req", axis=0, tiled=True),
        preferred_element_type=jnp.float32,
    )
    up_acc = jnp.dot(
        normed, lax.all_gather(w_up, "req", axis=0, tiled=True), preferred_element_type=jnp.float32
    )
    hidden = (jax.nn.silu(gate_acc) * up_acc).astype(jnp.bfloat16)
    return (hidden, cache_out)


def solution(mesh):
    in_specs = (
        P("req", "mp"),
        P("req", "mp"),
        P("req", "mp"),
        P("mp"),
        P("mp"),
        P("mp"),
        P("req"),
        P(),
        P(),
        P("mp", None),
        P("req", None),
        P(),
        P("req", "mp"),
        P("req", "mp"),
    )
    out_specs = (P("req", "mp"), P("req", "mp", None, None))
    return jax.shard_map(shards, mesh=mesh, in_specs=in_specs, out_specs=out_specs, check_vma=False)
```

profile of v0, /device:TPU:0, one launch (start us, length us, event | category | flops | bytes accessed | tf_op | source)
XLA Modules:
  0.0 873.2 jit_solution(3613381427273955708)
XLA Ops:
  9.6 2.6 gather_fusion.4
  15.3 3.5 gather_fusion
  20.5 7.3 all-to-all-start.1
  27.8 2.0 gather_fusion.1
  30.3 2.0 gather_fusion.3
  34.8 7.5 all-to-all-done.1
  42.3 3.6 all-to-all-start
  48.7 1.4 copy.102
  50.1 10.5 %all-to-all-done = bf16[8,128,256]{2,1,0:T(8,128)(2,1)S(1)} async-done(((bf16[8,128,256]{2,1,0:T(8,128)(2,1)}), bf16[8,128,256]{2,1,0:T(8,128)(2,1)S(1)}, u32[]{:S(2)}, u32[]{:S(2)}) %all-to-all-start) | async-done | bytes 524320 | tf_op jit(solution)/shard_map/all_to_all | solution.py:139
  60.6 3.8 all-to-all-start.2
  66.4 35.1 %all-to-all-done.2 = bf16[8,128,768]{2,1,0:T(8,128)(2,1)S(1)} async-done(((bf16[8,128,768]{2,1,0:T(8,128)(2,1)}), bf16[8,128,768]{2,1,0:T(8,128)(2,1)S(1)}, u32[]{:S(2)}, u32[]{:S(2)}) %all-to-all-start.2) | async-done | bytes 1572896 | tf_op jit(solution)/shard_map/all_to_all | solution.py:137
  101.5 1.6 copy.103
  103.0 5.0 fusion.53
  108.0 3.6 convolution_convert_fusion.1
  111.7 3.6 all-to-all-start.3
  115.5 36.9 %all-to-all-done.3 = bf16[8,128,768]{1,2,0:T(8,128)(2,1)S(1)} async-done(((bf16[8,128,768]{1,2,0:T(8,128)(2,1)}), bf16[8,128,768]{1,2,0:T(8,128)(2,1)S(1)}, u32[]{:S(2)}, u32[]{:S(2)}) %all-to-all-start.3) | async-done | bytes 1572896 | tf_op jit(solution)/shard_map/all_to_all | solution.py:147
  153.2 2.0 gather_fusion.2
  155.2 9.4 %convolution_convert_fusion = bf16[512,5120]{1,0:T(8,128)(2,1)} fusion(bf16[768,5120]{1,0:T(8,128)(2,1)} %param.25, bf16[512,768]{1,0:T(8,128)(2,1)S(1)} %gather_fusion.2, pred[512]{0:T(512)(128)(4,1)S(1)} %compare_and_fusion.2, pred[512]{0:T(512)(128)(4,1)S(1)} %broadcast_compare_fusion), kind=kOutput, calls=%fused_computation.9 | convolution fusion | flops 4029939712 | bytes 13894656 | tf_op jit(solution)/shard_map/dot_general | solution.py:163
  167.8 98.6 %all-reduce.2.cloned.1.call-done = bf16[512,5120]{1,0:T(8,128)(2,1)} async-done(((bf16[512,5120]{1,0:T(8,128)(2,1)}), bf16[512,5120]{1,0:T(8,128)(2,1)}) %all-reduce.2.cloned.1.call-update) | async-done | bytes 5242896 | tf_op jit(solution)/shard_map/psum | solution.py:162
  266.4 5.8 multiply_reduce_fusion
  272.2 233.8 %all-gather.3.cloned.1.call-done = bf16[5120,1728]{0,1:T(8,128)(2,1)} async-done(((bf16[640,1728]{0,1:T(8,128)(2,1)}), bf16[5120,1728]{0,1:T(8,128)(2,1)}) %all-gather.3.cloned.1.call-update) | async-done | bytes 17694736 | tf_op jit(solution)/shard_map/all_gather | solution.py:168
  506.0 17.7 %fusion.52 = f32[512,1728]{0,1:T(8,128)} fusion(bf16[5120,1728]{0,1:T(8,128)(2,1)} %all-gather.3.cloned.1.call-done, bf16[512,5120]{1,0:T(8,128)(2,1)} %all-reduce.2.cloned.1.call-done, bf16[512,5120]{1,0:T(8,128)(2,1)} %param.26, f32[5120]{0:T(1024)S(1)} %copy-done.12, f32[512]{0:T(512)S(1)} %add_rsqrt_fusion), kind=kOutput, calls=%fused_computation.123 | convolution fusion | flops 9075425280 | bytes 31741952 | tf_op jit(solution)/shard_map/dot_general | solution.py:166
  523.7 324.0 %all-gather.5.cloned.1.call-done = bf16[5120,1728]{0,1:T(8,128)(2,1)} async-done(((bf16[640,1728]{0,1:T(8,128)(2,1)}), bf16[5120,1728]{0,1:T(8,128)(2,1)}) %all-gather.5.cloned.1.call-update) | async-done | bytes 17694736 | tf_op jit(solution)/shard_map/all_gather | solution.py:172
  847.7 18.1 %fusion.3 = bf16[512,1728]{0,1:T(8,128)(2,1)} fusion(bf16[5120,1728]{0,1:T(8,128)(2,1)} %all-gather.5.cloned.1.call-done, f32[512,1728]{0,1:T(8,128)} %fusion.52, bf16[512,5120]{1,0:T(8,128)(2,1)} %all-reduce.2.cloned.1.call-done, bf16[512,5120]{1,0:T(8,128)(2,1)} %param.26, f32[5120]{0:T(1024)S(1)} %copy-done.12, f32[512]{0:T(512)S(1)} %add_rsqrt_fusion), kind=kOutput, calls=%fused_computation.16 | convolution fusion | flops 9080733696 | bytes 33511424 | tf_op jit(solution)/shard_map/dot_general | solution.py:171
  (91 shorter events, 17.9 us)
Async XLA Ops:
  8.0 19.7 %copy-start = (bf16[512,768]{1,0:T(8,128)(2,1)S(1)}, bf16[512,768]{1,0:T(8,128)(2,1)}, u32[]{:S(2)}) copy-start(bf16[512,768]{1,0:T(8,128)(2,1)} %param.16) | copy-start | bytes 2359300
  9.6 5.7 copy-start.2
  20.5 21.9 %all-to-all-start.1 = ((bf16[8,128,256]{2,1,0:T(8,128)(2,1)}), bf16[8,128,256]{2,1,0:T(8,128)(2,1)}, u32[]{:S(2)}, u32[]{:S(2)}) async-start(bf16[8,128,256]{2,1,0:T(8,128)(2,1)} %copy.97), calls=%async_computation.1 | async-start | bytes 1048576 | tf_op jit(solution)/shard_map/all_to_all | solution.py:138
  27.7 2.5 copy-start.3
  29.8 2.5 copy-start.11
  30.1 3.7 copy-start.10
  42.3 18.3 %all-to-all-start = ((bf16[8,128,256]{2,1,0:T(8,128)(2,1)}), bf16[8,128,256]{2,1,0:T(8,128)(2,1)S(1)}, u32[]{:S(2)}, u32[]{:S(2)}) async-start(bf16[8,128,256]{2,1,0:T(8,128)(2,1)} %copy.92), calls=%async_computation | async-start | bytes 1048576 | tf_op jit(solution)/shard_map/all_to_all | solution.py:139
  48.7 15.8 %copy-start.8 = (s32[8,4]{0,1:T(4,128)S(1)}, s32[8,4]{0,1:T(4,128)}, u32[]{:S(2)}) copy-start(s32[8,4]{0,1:T(4,128)} %param.24) | copy-start | bytes 388
  48.7 15.8 %copy-start.9 = (s32[8,4]{0,1:T(4,128)S(1)}, s32[8,4]{0,1:T(4,128)}, u32[]{:S(2)}) copy-start(s32[8,4]{0,1:T(4,128)} %param.23) | copy-start | bytes 388
  60.6 40.8 %all-to-all-start.2 = ((bf16[8,128,768]{2,1,0:T(8,128)(2,1)}), bf16[8,128,768]{2,1,0:T(8,128)(2,1)S(1)}, u32[]{:S(2)}, u32[]{:S(2)}) async-start(bf16[8,128,768]{2,1,0:T(8,128)(2,1)} %copy.102), calls=%async_computation.2 | async-start | bytes 3145728 | tf_op jit(solution)/shard_map/all_to_all | solution.py:137
  66.1 41.9 %copy-start.4 = (bf16[8,128,256]{1,2,0:T(8,128)(2,1)}, bf16[8,128,256]{1,2,0:T(8,128)(2,1)S(1)}, u32[]{:S(2)}) copy-start(bf16[8,128,256]{1,2,0:T(8,128)(2,1)S(1)} %copy.98) | copy-start | bytes 1572868
  66.4 41.6 %copy-start.6 = (bf16[8,128,256]{1,2,0:T(8,128)(2,1)}, bf16[8,128,256]{1,2,0:T(8,128)(2,1)S(1)}, u32[]{:S(2)}) copy-start(bf16[8,128,256]{1,2,0:T(8,128)(2,1)S(1)} %copy.93) | copy-start | bytes 1572868
  111.7 40.8 %all-to-all-start.3 = ((bf16[8,128,768]{1,2,0:T(8,128)(2,1)}), bf16[8,128,768]{1,2,0:T(8,128)(2,1)S(1)}, u32[]{:S(2)}, u32[]{:S(2)}) async-start(bf16[8,128,768]{1,2,0:T(8,128)(2,1)} %bitcast.90), calls=%async_computation.3 | async-start | bytes 3145728 | tf_op jit(solution)/shard_map/all_to_all | solution.py:147
  115.3 151.1 %all-reduce.2.cloned.1.call-start = ((), (), s32[]{:S(2)}) async-start(), calls=%async_computation.4 | async-start | bytes 10485760 | tf_op jit(solution)/shard_map/psum | solution.py:162
  164.6 1.3 copy-start.5
  164.6 1.6 copy-start.7
  164.6 341.4 %all-gather.3.cloned.1.call-start = ((), (), s32[]{:S(2)}) async-start(), calls=%async_computation.5 | async-start | bytes 19906560 | tf_op jit(solution)/shard_map/all_gather | solution.py:168
  165.2 682.5 %all-gather.5.cloned.1.call-start = ((), (), s32[]{:S(2)}) async-start(), calls=%async_computation.6 | async-start | bytes 19906560 | tf_op jit(solution)/shard_map/all_gather | solution.py:172
  167.8 338.2 %copy-start.12 = (f32[5120]{0:T(1024)S(1)}, f32[5120]{0:T(1024)}, u32[]{:S(2)}) copy-start(f32[5120]{0:T(1024)} %param.27) | copy-start | bytes 61444
  847.7 18.1 %copy-start.1 = (bf16[512,768]{1,0:T(8,128)(2,1)S(1)}, bf16[512,768]{1,0:T(8,128)(2,1)}, u32[]{:S(2)}) copy-start(bf16[512,768]{1,0:T(8,128)(2,1)} %param.16) | copy-start | bytes 2359300
Sparse Core Ops, SparseCore 0:
  164.7 101.6 all-reduce.1
Sparse Core Ops, SparseCore 1:
  166.6 339.3 all-gather.2
  507.4 340.2 all-gather.4
where the time goes:
time: 874 us; the launch traced here: 873 us
  waiting for transfers between devices  747 us (85%)
  matrix products  55.9 us (6%)
  local copies, waits for them, and re-layouts  22.8 us (3%)
  starting transfers between devices  18.6 us (2%)
  between operations  16 us (2%)
  other arithmetic  12.6 us (1%)
    all_gather x1, waiting for transfers between devices, shards(): lax.all_gather(w_up, 'req', axis=0, tiled=True)  324 us
    all_gather x1, waiting for transfers between devices, shards(): lax.all_gather(w_gate, 'req', axis=0, tiled=True)  234 us
    psum x1, waiting for transfers between devices, shards(): lax.psum(jnp.dot(attn_rows, w_out, preferred_element_type=jnp.float32).as...  98.6 us
    all_to_all x1, waiting for transfers between devices, shards(): lax.all_to_all(attended.reshape(groups_all, PAGE, q_heads * HD), 'req', s...  36.9 us
    all_to_all x1, waiting for transfers between devices, shards(): lax.all_to_all(q_send, 'req', split_axis=0, concat_axis=0, tiled=True)  35.1 us
    dot_general x1, matrix products, shards(): jnp.dot(normed, lax.all_gather(w_up, 'req', axis=0, tiled=True), preferre...  18.1 us
    dot_general x1, matrix products, shards(): jnp.dot(normed, lax.all_gather(w_gate, 'req', axis=0, tiled=True), prefer...  17.7 us
  transfers between devices with their start and end apart: 7, of which 7 were waited for; matrix products, arithmetic and copies ran while one was open for 4% of the time, Pallas kernels for 0%

commit v1 on v0

v1 whole, which is shorter than its diff:
```python
import math

import jax
import jax.numpy as jnp
from jax import lax
from jax.experimental import pallas as pl
from jax.experimental.pallas import tpu as pltpu
from jax.sharding import PartitionSpec as P

HD = 128
PAGE = 128
REQS = 4
CORES = 2
THETA = 1000000.0
EPS = 1e-06
NT = (((1,), (1,)), ((), ()))


def rope_tables(positions):
    half_dim = HD // 2
    frequencies = THETA ** (-jnp.arange(half_dim, dtype=jnp.float32) * (2.0 / HD))
    angles = positions[:, None] * frequencies[None, :]
    cosine = jnp.cos(angles)
    sine = jnp.sin(angles)
    return jnp.concatenate([cosine, cosine], axis=-1), jnp.concatenate([-sine, sine], axis=-1)


def attention_kernel(q_ref, k_ref, v_ref, qb_ref, kb_ref, vb_ref, cos_ref, sin_ref, segc_ref, segr_ref,
                     slot_ref, out_ref, send_ref, q_buf, k_buf, v_buf, kv_buf):
    rows = q_ref.shape[0]
    kv_heads = k_ref.shape[1] // HD
    q_heads = q_ref.shape[1] // HD
    group = q_heads // kv_heads
    live = segc_ref[...] >= 0
    cosine = cos_ref[...]
    sine = sin_ref[...]

    def turned(source, bias, head):
        cols = slice(head * HD, (head + 1) * HD)
        raw = source[:, cols].astype(jnp.float32) + bias[:, cols]
        return jnp.where(live, raw * cosine + pltpu.roll(raw, HD // 2, 1) * sine, 0.0).astype(jnp.bfloat16)

    for head in range(q_heads):
        q_buf[:, head * HD:(head + 1) * HD] = turned(q_ref, qb_ref, head)
    for head in range(kv_heads):
        cols = slice(head * HD, (head + 1) * HD)
        key = turned(k_ref, kb_ref, head)
        value = jnp.where(live, v_ref[:, cols].astype(jnp.float32) + vb_ref[:, cols], 0.0).astype(jnp.bfloat16)
        k_buf[:, cols] = key
        v_buf[:, cols] = value
        kv_buf[:, 2 * head * HD:(2 * head + 1) * HD] = key
        kv_buf[:, (2 * head + 1) * HD:(2 * head + 2) * HD] = value
    slots = slot_ref[...]
    for part in range(send_ref.shape[0] // rows):
        wanted = lax.broadcasted_iota(jnp.int32, (rows, rows), 0) + part * rows
        pick = jnp.where(wanted == slots, 1.0, 0.0).astype(jnp.bfloat16)
        send_ref[part * rows:(part + 1) * rows, :] = jnp.dot(
            pick, kv_buf[...], preferred_element_type=jnp.float32
        ).astype(jnp.bfloat16)
    scale = 1.0 / math.sqrt(HD)
    tile = PAGE
    for start in range(0, rows, tile):
        low = max(0, start - tile)
        high = start + tile
        seg_q = segc_ref[start:high, :]
        seg_k = segr_ref[:, low:high]
        row_at = lax.broadcasted_iota(jnp.int32, (tile, high - low), 0) + start
        col_at = lax.broadcasted_iota(jnp.int32, (tile, high - low), 1) + low
        allowed = (seg_q == seg_k) & (seg_k >= 0) & (col_at <= row_at)
        for head in range(q_heads):
            kv = head // group
            kv_cols = slice(kv * HD, (kv + 1) * HD)
            scores = lax.dot_general(
                q_buf[start:high, head * HD:(head + 1) * HD], k_buf[low:high, kv_cols], NT,
                preferred_element_type=jnp.float32,
            ) * scale
            row_max = jnp.max(jnp.where(allowed, scores, -1e30), axis=-1, keepdims=True)
            weights = jnp.where(allowed, jnp.exp(scores - row_max), 0.0)
            total = jnp.sum(weights, axis=-1, keepdims=True)
            probs = (weights / jnp.where(total > 0.0, total, 1.0)).astype(jnp.bfloat16)
            out_ref[start:high, head * HD:(head + 1) * HD] = jnp.dot(
                probs, v_buf[low:high, kv_cols], preferred_element_type=jnp.float32
            ).astype(jnp.bfloat16)


def attention(q_pre, k_pre, v_pre, q_bias, k_bias, v_bias, cosine, sine, segs, slots, slot_count):
    rows, q_cols = q_pre.shape
    kv_cols = k_pre.shape[1]
    vmem = pl.BlockSpec(memory_space=pltpu.VMEM)
    return pl.pallas_call(
        attention_kernel,
        out_shape=(
            jax.ShapeDtypeStruct((rows, q_cols), jnp.bfloat16),
            jax.ShapeDtypeStruct((slot_count, 2 * kv_cols), jnp.bfloat16),
        ),
        in_specs=[vmem] * 11,
        out_specs=(vmem, vmem),
        scratch_shapes=[
            pltpu.VMEM((rows, q_cols), jnp.bfloat16),
            pltpu.VMEM((rows, kv_cols), jnp.bfloat16),
            pltpu.VMEM((rows, kv_cols), jnp.bfloat16),
            pltpu.VMEM((rows, 2 * kv_cols), jnp.bfloat16),
        ],
        compiler_params=pltpu.CompilerParams(vmem_limit_bytes=32 * 2**20),
        cost_estimate=pl.CostEstimate(flops=2 * 10**9, bytes_accessed=4 * 2**20, transcendentals=10**6),
        name="attention",
    )(q_pre, k_pre, v_pre, q_bias[None], k_bias[None], v_bias[None], cosine, sine, segs[:, None], segs[None],
      slots[None])


def cache_kernel(source_ref, in_ref, out_ref):
    out_ref[0, 0] = in_ref[0]


def write_cache(sources, pages_in, kv_heads):
    grid_spec = pltpu.PrefetchScalarGridSpec(
        num_scalar_prefetch=1,
        grid=(REQS, kv_heads),
        in_specs=[pl.BlockSpec((1, PAGE, 2 * HD), lambda page, head, source: (source[page], 0, head))],
        out_specs=pl.BlockSpec((1, 1, PAGE, 2 * HD), lambda page, head, source: (page, head, 0, 0)),
    )
    return pl.pallas_call(
        cache_kernel,
        out_shape=jax.ShapeDtypeStruct((REQS, kv_heads, PAGE, 2 * HD), jnp.bfloat16),
        grid_spec=grid_spec,
        name="write_cache",
    )(sources, pages_in)


def mlp_kernel(count, pieces, ids_ref, *refs):
    weights = refs[:count]
    rows_in = refs[count:count + pieces]
    out_ref, gate_buf, up_buf, row_buf, weight_sems, row_sems = refs[count + pieces:]
    depth = weights[0].shape[2]
    piece = rows_in[0].shape[0]
    copies = []
    for index in range(pieces):
        at = pl.multiple_of(ids_ref[count + index] * piece, piece)
        copies.append(pltpu.make_async_copy(rows_in[index], row_buf.at[pl.ds(at, piece), :], row_sems.at[index]))
    for index in range(count):
        at = pl.multiple_of(ids_ref[index] * depth, depth)
        for which, buf in enumerate((gate_buf, up_buf)):
            copies.append(
                pltpu.make_async_copy(
                    weights[index].at[which], buf.at[:, pl.ds(at, depth)], weight_sems.at[which, index]
                )
            )
    for copy in copies:
        copy.start()
    for copy in copies:
        copy.wait()
    tile = min(256, out_ref.shape[1])
    for start in range(0, out_ref.shape[1], tile):
        block = row_buf[start:start + tile, :]
        gate = lax.dot_general(gate_buf[...], block, NT, preferred_element_type=jnp.float32)
        up = lax.dot_general(up_buf[...], block, NT, preferred_element_type=jnp.float32)
        out_ref[:, start:start + tile] = (gate / (1.0 + jnp.exp(-gate)) * up).astype(jnp.bfloat16)


def mlp_block(weights, weight_ids, rows_in, row_ids):
    count, pieces = len(weights), len(rows_in)
    units, depth = weights[0].shape[1:]
    piece, width = rows_in[0].shape
    tokens = piece * pieces
    if depth % 128 or units % 16 or piece % 16:
        both = jnp.zeros((2, units, width), jnp.bfloat16)
        for index in range(count):
            both = lax.dynamic_update_slice(both, weights[index], (0, 0, weight_ids[index] * depth))
        rows = jnp.zeros((tokens, width), jnp.bfloat16)
        for index in range(pieces):
            rows = lax.dynamic_update_slice(rows, rows_in[index], (row_ids[index] * piece, 0))
        gate = lax.dot_general(both[0], rows, NT, preferred_element_type=jnp.float32)
        up = lax.dot_general(both[1], rows, NT, preferred_element_type=jnp.float32)
        return (jax.nn.silu(gate) * up).astype(jnp.bfloat16)
    ids = jnp.stack([jnp.asarray(i, jnp.int32) for i in list(weight_ids) + list(row_ids)])
    anywhere = pl.BlockSpec(memory_space=pl.ANY)
    return pl.pallas_call(
        lambda *refs: mlp_kernel(count, pieces, *refs),
        out_shape=jax.ShapeDtypeStruct((units, tokens), jnp.bfloat16),
        in_specs=[pl.BlockSpec(memory_space=pltpu.SMEM)] + [anywhere] * (count + pieces),
        out_specs=pl.BlockSpec(memory_space=pltpu.VMEM),
        scratch_shapes=[
            pltpu.VMEM((units, width), jnp.bfloat16),
            pltpu.VMEM((units, width), jnp.bfloat16),
            pltpu.VMEM((tokens, width), jnp.bfloat16),
            pltpu.SemaphoreType.DMA((2, count)),
            pltpu.SemaphoreType.DMA((pieces,)),
        ],
        compiler_params=pltpu.CompilerParams(vmem_limit_bytes=48 * 2**20),
        cost_estimate=pl.CostEstimate(
            flops=4 * units * width * tokens,
            bytes_accessed=2 * (2 * units * width + tokens * width + units * tokens),
            transcendentals=units * tokens,
        ),
        name="mlp_block",
    )(ids, *weights, *rows_in)


def shards(q_pre, k_pre, v_pre, q_bias, k_bias, v_bias, segment_ids, lengths, page_table, w_out, residual,
           norm_gain, w_gate, w_up):
    me_req = lax.axis_index("req")
    me_mp = lax.axis_index("mp")
    n_req = lax.axis_size("req")
    n_mp = lax.axis_size("mp")
    n_z = 4 if n_req % 4 == 0 else 1
    n_y = n_req // n_z
    n_x = n_mp // CORES
    z = me_req // n_y
    y = me_req % n_y
    x = me_mp // CORES
    core = me_mp % CORES

    def along_z(value, shift):
        pairs = [(a * n_y + b, (a + shift) % n_z * n_y + b) for a in range(n_z) for b in range(n_y)]
        return lax.ppermute(value, "req", pairs)

    def along_y(value, shift):
        pairs = [(a * n_y + b, a * n_y + (b + shift) % n_y) for a in range(n_z) for b in range(n_y)]
        return lax.ppermute(value, "req", pairs)

    def along_x(value, shift):
        pairs = [(a * CORES + b, (a + shift) % n_x * CORES + b) for a in range(n_x) for b in range(CORES)]
        return lax.ppermute(value, "mp", pairs)

    def across_cores(value):
        pairs = [(a * CORES + b, a * CORES + 1 - b) for a in range(n_x) for b in range(CORES)]
        return lax.ppermute(value, "mp", pairs)

    units_all, depth = w_gate.shape[1], w_gate.shape[0]
    units = units_all // n_z
    gate_t, up_t = w_gate.T, w_up.T

    def share(target):
        at = (target * units, 0)
        return jnp.stack(
            [lax.dynamic_slice(gate_t, at, (units, depth)), lax.dynamic_slice(up_t, at, (units, depth))]
        )

    weights, weight_ids = [], []

    def arrived(chunk, shift):
        source_z = (z - shift) % n_z
        weights.append(chunk)
        weight_ids.append(source_z * n_y + y)
        for step in range(1, n_y):
            weights.append(along_y(chunk, step))
            weight_ids.append(source_z * n_y + (y - step) % n_y)

    arrived(share(z), 0)
    last = None
    shifts = [n_z // 2] + [s for s in range(1, n_z) if s != n_z // 2]
    for shift in shifts if n_z > 1 else []:
        chunk = share((z + shift) % n_z)
        if last is not None:
            chunk, last = lax.optimization_barrier((chunk, last))
        last = along_z(chunk, shift)
        arrived(last, shift)

    rows = q_pre.shape[0]
    kv_heads = k_pre.shape[1] // HD
    own_lens = lax.dynamic_index_in_dim(lengths, me_req, 0, keepdims=False)
    own_pages = lax.dynamic_index_in_dim(page_table, me_req, 0, keepdims=False)
    own_owner = own_pages // REQS
    starts = jnp.cumsum(own_lens) - own_lens
    alive = segment_ids >= 0
    req_idx = jnp.clip(segment_ids - me_req * REQS, 0, REQS - 1)
    hit = req_idx[:, None] == jnp.arange(REQS)[None, :]
    row_start = jnp.sum(jnp.where(hit, starts[None, :], 0), axis=1)
    row_owner = jnp.sum(jnp.where(hit, own_owner[None, :], 0), axis=1)
    row_pos = jnp.arange(rows, dtype=jnp.int32) - row_start
    slots = jnp.where(alive, row_owner * PAGE + row_pos, -1)
    cosine, sine = rope_tables(row_pos.astype(jnp.float32))
    attended, kv_send = attention(
        q_pre, k_pre, v_pre, q_bias, k_bias, v_bias, cosine, sine, segment_ids, slots, n_req * PAGE
    )
    partial = jnp.dot(attended, w_out, preferred_element_type=jnp.float32).astype(jnp.bfloat16)
    width = partial.shape[1]
    piece = rows // n_mp
    parts = lax.all_to_all(partial.reshape(n_mp, piece, width), "mp", split_axis=0, concat_axis=0, tiled=True)
    summed = jnp.sum(parts.astype(jnp.float32), axis=0)
    state = lax.dynamic_slice(residual, (me_mp * piece, 0), (piece, width)).astype(jnp.float32) + summed
    scale = lax.rsqrt(jnp.mean(state * state, axis=-1, keepdims=True) + EPS)
    normed = (state * scale * norm_gain).astype(jnp.bfloat16)

    kv_in = lax.all_to_all(
        kv_send.reshape(n_req, PAGE, 2 * kv_heads * HD), "req", split_axis=0, concat_axis=0, tiled=True
    )
    mine = page_table[None] == (me_req * REQS + jnp.arange(REQS, dtype=jnp.int32))[:, None, None]
    sources = jnp.sum(jnp.where(mine, jnp.arange(n_req, dtype=jnp.int32)[None, :, None], 0), axis=(1, 2))
    cache_out = write_cache(sources.astype(jnp.int32), kv_in, kv_heads)

    def spread(own):
        across = [(own, x)] + [(along_x(own, step), (x - step) % n_x) for step in range(1, n_x)]
        pieces = [(value, at * CORES + core) for value, at in across]
        pieces += [(across_cores(value), at * CORES + 1 - core) for value, at in across]
        return [p[0] for p in pieces], [p[1] for p in pieces]

    normed, last = lax.optimization_barrier((normed, last)) if last is not None else (normed, None)
    hidden_t = jnp.zeros((units_all, rows), jnp.bfloat16)
    block = normed
    for step in range(n_z):
        if step:
            block = along_z(block, 1)
        values, at = spread(block)
        done = mlp_block(weights, weight_ids, values, at)
        if step:
            done = along_z(done, -step)
        hidden_t = lax.dynamic_update_slice(hidden_t, done, ((z + step) % n_z * units, 0))
    return hidden_t.T, cache_out


def solution(mesh):
    in_specs = (
        P("req", "mp"),
        P("req", "mp"),
        P("req", "mp"),
        P("mp"),
        P("mp"),
        P("mp"),
        P("req"),
        P(),
        P(),
        P("mp", None),
        P("req", None),
        P(),
        P("req", "mp"),
        P("req", "mp"),
    )
    out_specs = (P("req", "mp"), P("req", "mp", None, None))
    return jax.shard_map(shards, mesh=mesh, in_specs=in_specs, out_specs=out_specs, check_vma=False)
```

time: 874 us -> 372 us (0.43)
  waiting for transfers between devices: 747 us -> 254 us
  matrix products: 55.9 us -> 6.07 us
  Pallas kernels: 0 us -> 46.3 us
  starting transfers between devices: 18.6 us -> 35.3 us
  between operations: 16 us -> 1.12 us
  local copies, waits for them, and re-layouts: 22.8 us -> 13.2 us
    all_gather x2 -> x0, waiting for transfers between devices: 558 us -> none  [the longest x1 324 us: shards(): lax.all_gather(w_up, 'req', axis=0, tiled=True)]
    ppermute x0 -> x25, waiting for transfers between devices: none -> 254 us  [the longest x9 158 us: along_z(): return lax.ppermute(value, 'req', pairs)]
    psum x1 -> x0, waiting for transfers between devices: 98.6 us -> none  [shards(): lax.psum(jnp.dot(attn_rows, w_out, preferred_element_type=jnp.float32).as...]
    all_to_all x4 -> x2, waiting for transfers between devices: 90.1 us -> 0.01 us  [the longest x1 0.01 us: shards(): lax.all_to_all(partial.reshape(n_mp, piece, width), 'mp', split_axis=0, c...]
    pallas_call x0 -> x6, Pallas kernels: none -> 46.3 us  [the longest x4 36.3 us: mlp_block(): pl.pallas_call(lambda *refs: mlp_kernel(count, pieces, *refs), out_shape=...]
    dot_general x8 -> x1, matrix products: 51 us -> 6.07 us  [shards(): jnp.dot(attended, w_out, preferred_element_type=jnp.float32)]
    ppermute x0 -> x25, starting transfers between devices: none -> 24.2 us  [the longest x9 11.1 us: along_z(): return lax.ppermute(value, 'req', pairs)]
    gather x7 -> x0, local copies, waits for them, and re-layouts: 12.5 us -> none  [the longest x5 6.99 us: prepare(): picked = jnp.take(source, flat_index, axis=0).astype(jnp.float32) + bias_row]
  transfers between devices with their start and end apart: 7 -> 27, of which waited for: 7 -> 11; matrix products, arithmetic and copies ran while one was open for 4% -> 4% of each run, Pallas kernels for 0% -> 11%
where the time goes in v1:
time: 372 us; the launch traced here: 371 us
  waiting for transfers between devices  254 us (68%)
  Pallas kernels  46.3 us (12%)
  starting transfers between devices  35.3 us (9%)
  other arithmetic  15.5 us (4%)
  local copies, waits for them, and re-layouts  13.2 us (4%)
  matrix products  6.07 us (2%)
    ppermute x9, waiting for transfers between devices, along_z(): return lax.ppermute(value, 'req', pairs)  158 us
    ppermute x4, waiting for transfers between devices, along_y(): return lax.ppermute(value, 'req', pairs)  59.3 us
    ppermute x4, waiting for transfers between devices, along_x(): return lax.ppermute(value, 'mp', pairs)  36.6 us
    pallas_call x4, Pallas kernels, mlp_block(): pl.pallas_call(lambda *refs: mlp_kernel(count, pieces, *refs), out_shape=...  36.3 us
    ppermute x9, starting transfers between devices, along_z(): return lax.ppermute(value, 'req', pairs)  11.1 us
  transfers between devices with their start and end apart: 27, of which 11 were waited for; matrix products, arithmetic and copies ran while one was open for 4% of the time, Pallas kernels for 11%

profile of v1, /device:TPU:0, one launch (start us, length us, event | category | flops | bytes accessed | tf_op | source)
XLA Modules:
  0.0 371.1 jit_solution(2569159522783674502)
XLA Ops:
  6.9 4.5 %attention.1 = (bf16[512,768]{1,0:T(8,128)(2,1)S(1)}, bf16[1024,512]{1,0:T(8,128)(2,1)}) custom-call(bf16[512,768]{1,0:T(8,128)(2,1)S(1)} %copy-done.6, bf16[512,256]{1,0:T(8,128)(2,1)S(1)} %copy-done.7, bf16[512,256]{1,0:T(8,128)(2,1)S(1)} %copy-done.8, f32[1,768]{1,0:T(1,128)S(1)} %broadcast_in_dim.71.qb_ref, f32[1,256]{1,0:T(1,128)S(1)} %bitcast.57, ...), custom_call_target="tpu_custom_call" | custom-call | flops 2000000000 | bytes 4194304 | tf_op jit(solution)/shard_map/attention/pallas_call | solution.py:90
  11.4 6.1 %convolution_convert_fusion = bf16[512,5120]{1,0:T(8,128)(2,1)} fusion(bf16[512,768]{1,0:T(8,128)(2,1)S(1)} %get-tuple-element.9, bf16[768,5120]{1,0:T(8,128)(2,1)S(1)} %copy-done.16), kind=kOutput, calls=%fused_computation.1 | convolution fusion | flops 4029153280 | bytes 13893632 | tf_op jit(solution)/shard_map/dot_general | solution.py:276
  17.5 5.1 %all-to-all-start = ((bf16[4,128,5120]{2,1,0:T(8,128)(2,1)}), bf16[4,128,5120]{2,1,0:T(8,128)(2,1)}, u32[]{:S(2)}, u32[]{:S(2)}) async-start(bf16[4,128,5120]{2,1,0:T(8,128)(2,1)} %bitcast.59), calls=%async_computation | async-start | bytes 10485760 | tf_op jit(solution)/shard_map/all_to_all | solution.py:279
  22.6 3.6 dynamic-slice_bitcast_fusion
  26.4 4.1 %collective-permute-start.1 = (bf16[2,432,640]{2,1,0:T(8,128)(2,1)S(1)}, bf16[2,432,640]{2,1,0:T(8,128)(2,1)S(1)}, u32[]{:S(2)}, u32[]{:S(2)}) collective-permute-start(bf16[2,432,640]{2,1,0:T(8,128)(2,1)S(1)} %pad_maximum_fusion.1), channel_id=1, source_target_pairs={{0,16},{4,20},{8,24},{12,28},{16,0},{20,4},{24,8},{28,12},{1,17},{... | collective-permute-start | bytes 3317768 | tf_op jit(solution)/shard_map/ppermute | solution.py:215
  31.6 47.5 %collective-permute-done.1.refs_3_ = bf16[2,432,640]{2,1,0:T(8,128)(2,1)S(1)} collective-permute-done((bf16[2,432,640]{2,1,0:T(8,128)(2,1)S(1)}, bf16[2,432,640]{2,1,0:T(8,128)(2,1)S(1)}, u32[]{:S(2)}, u32[]{:S(2)}) %collective-permute-start.1) | collective-permute-done | bytes 1105952 | tf_op jit(solution)/shard_map/ppermute | solution.py:215
  80.9 26.5 %collective-permute-done.3.refs_5_ = bf16[2,432,640]{2,1,0:T(8,128)(2,1)S(1)} collective-permute-done((bf16[2,432,640]{2,1,0:T(8,128)(2,1)}, bf16[2,432,640]{2,1,0:T(8,128)(2,1)S(1)}, u32[]{:S(2)}, u32[]{:S(2)}) %collective-permute-start.3) | collective-permute-done | bytes 1105952 | tf_op jit(solution)/shard_map/ppermute | solution.py:215
  109.2 3.8 %convert_reduce_fusion = f32[128,5120]{1,0:T(8,128)S(1)} fusion(bf16[4,128,5120]{2,1,0:T(8,128)(2,1)} %all-to-all-done), kind=kLoop, calls=%fused_computation | loop fusion | flops 4587520 | bytes 7864320 | tf_op jit(solution)/shard_map/reduce_sum | solution.py:280
  117.7 15.5 %collective-permute-done.5.refs_7_ = bf16[2,432,640]{2,1,0:T(8,128)(2,1)} collective-permute-done((bf16[2,432,640]{2,1,0:T(8,128)(2,1)}, bf16[2,432,640]{2,1,0:T(8,128)(2,1)}, u32[]{:S(2)}, u32[]{:S(2)}) %collective-permute-start.5) | collective-permute-done | bytes 1105952 | tf_op jit(solution)/shard_map/ppermute | solution.py:215
  133.3 31.1 %collective-permute-done.10.refs_9_ = bf16[128,5120]{1,0:T(8,128)(2,1)} collective-permute-done((bf16[128,5120]{1,0:T(8,128)(2,1)}, bf16[128,5120]{1,0:T(8,128)(2,1)}, u32[]{:S(2)}, u32[]{:S(2)}) %collective-permute-start.10) | collective-permute-done | bytes 1310752 | tf_op jit(solution)/shard_map/ppermute | solution.py:215
  168.1 26.4 %collective-permute-done.15.refs_9_ = bf16[128,5120]{1,0:T(8,128)(2,1)} collective-permute-done((bf16[128,5120]{1,0:T(8,128)(2,1)}, bf16[128,5120]{1,0:T(8,128)(2,1)}, u32[]{:S(2)}, u32[]{:S(2)}) %collective-permute-start.15) | collective-permute-done | bytes 1310752 | tf_op jit(solution)/shard_map/ppermute | solution.py:215
  198.7 16.9 %collective-permute-done.2.refs_4_ = bf16[2,432,640]{2,1,0:T(8,128)(2,1)S(1)} collective-permute-done((bf16[2,432,640]{2,1,0:T(8,128)(2,1)S(1)}, bf16[2,432,640]{2,1,0:T(8,128)(2,1)S(1)}, u32[]{:S(2)}, u32[]{:S(2)}) %collective-permute-start.2) | collective-permute-done | bytes 1105952 | tf_op jit(solution)/shard_map/ppermute | solution.py:219
  218.2 21.1 %collective-permute-done.4.refs_6_ = bf16[2,432,640]{2,1,0:T(8,128)(2,1)S(1)} collective-permute-done((bf16[2,432,640]{2,1,0:T(8,128)(2,1)S(1)}, bf16[2,432,640]{2,1,0:T(8,128)(2,1)S(1)}, u32[]{:S(2)}, u32[]{:S(2)}) %collective-permute-start.4) | collective-permute-done | bytes 1105952 | tf_op jit(solution)/shard_map/ppermute | solution.py:219
  241.9 6.0 %all-to-all-start.1 = ((bf16[8,128,512]{2,1,0:T(8,128)(2,1)}), bf16[8,128,512]{2,1,0:T(8,128)(2,1)}, u32[]{:S(2)}, u32[]{:S(2)}) async-start(bf16[8,128,512]{2,1,0:T(8,128)(2,1)} %bitcast.35), calls=%async_computation.1 | async-start | bytes 2097152 | tf_op jit(solution)/shard_map/all_to_all | solution.py:285
  247.9 21.3 %collective-permute-done.6.refs_8_ = bf16[2,432,640]{2,1,0:T(8,128)(2,1)} collective-permute-done((bf16[2,432,640]{2,1,0:T(8,128)(2,1)}, bf16[2,432,640]{2,1,0:T(8,128)(2,1)}, u32[]{:S(2)}, u32[]{:S(2)}) %collective-permute-start.6) | collective-permute-done | bytes 1105952 | tf_op jit(solution)/shard_map/ppermute | solution.py:219
  271.4 13.9 %collective-permute-done.16.refs_10_ = bf16[128,5120]{1,0:T(8,128)(2,1)} collective-permute-done((bf16[128,5120]{1,0:T(8,128)(2,1)}, bf16[128,5120]{1,0:T(8,128)(2,1)}, u32[]{:S(2)}, u32[]{:S(2)}) %collective-permute-start.16) | collective-permute-done | bytes 1310752 | tf_op jit(solution)/shard_map/ppermute | solution.py:223
  285.8 22.7 %collective-permute-done.21.refs_10_ = bf16[128,5120]{1,0:T(8,128)(2,1)} collective-permute-done((bf16[128,5120]{1,0:T(8,128)(2,1)}, bf16[128,5120]{1,0:T(8,128)(2,1)}, u32[]{:S(2)}, u32[]{:S(2)}) %collective-permute-start.21) | collective-permute-done | bytes 1310752 | tf_op jit(solution)/shard_map/ppermute | solution.py:223
  310.0 5.4 %write_cache.1 = bf16[4,2,128,256]{3,2,1,0:T(8,128)(2,1)} custom-call(s32[4]{0:T(128)} %select_reduce_fusion.source_ref, bf16[8,128,512]{2,1,0:T(8,128)(2,1)} %all-to-all-done.1.in_ref), custom_call_target="tpu_custom_call" | custom-call | tf_op jit(solution)/shard_map/write_cache/pallas_call | solution.py:122
  317.9 9.1 %mlp_block.5 = bf16[432,512]{1,0:T(8,128)(2,1)S(1)} custom-call(s32[12]{0:T(128)S(1)} %stack.62.refs_0_, bf16[2,432,640]{2,1,0:T(8,128)(2,1)S(1)} %pad_maximum_fusion.refs_1_, bf16[2,432,640]{2,1,0:T(8,128)(2,1)S(1)} %copy-done.2, bf16[2,432,640]{2,1,0:T(8,128)(2,1)S(1)} %collective-permute-done.1.refs_3_, bf16[2,432,640]{2,1,0:T(8,128)(2,1)S(1)} %copy-done.4, ...), custom_call_target="tpu_custom_call" | custom-call | flops 4529848320 | bytes 14532608 | tf_op jit(solution)/shard_map/mlp_block/pallas_call | solution.py:177
  327.0 3.6 collective-permute-start.14
  330.6 9.1 %mlp_block.6 = bf16[432,512]{1,0:T(8,128)(2,1)S(1)} custom-call(s32[12]{0:T(128)S(1)} %stack.62.refs_0_, bf16[2,432,640]{2,1,0:T(8,128)(2,1)S(1)} %pad_maximum_fusion.refs_1_, bf16[2,432,640]{2,1,0:T(8,128)(2,1)S(1)} %copy-done.2, bf16[2,432,640]{2,1,0:T(8,128)(2,1)S(1)} %collective-permute-done.1.refs_3_, bf16[2,432,640]{2,1,0:T(8,128)(2,1)S(1)} %copy-done.4, ...), custom_call_target="tpu_custom_call" | custom-call | flops 4529848320 | bytes 14532608 | tf_op jit(solution)/shard_map/mlp_block/pallas_call | solution.py:177
  339.8 9.1 %mlp_block.7 = bf16[432,512]{1,0:T(8,128)(2,1)S(1)} custom-call(s32[12]{0:T(128)S(1)} %stack.62.refs_0_, bf16[2,432,640]{2,1,0:T(8,128)(2,1)S(1)} %pad_maximum_fusion.refs_1_, bf16[2,432,640]{2,1,0:T(8,128)(2,1)S(1)} %copy-done.2, bf16[2,432,640]{2,1,0:T(8,128)(2,1)S(1)} %collective-permute-done.1.refs_3_, bf16[2,432,640]{2,1,0:T(8,128)(2,1)S(1)} %copy-done.4, ...), custom_call_target="tpu_custom_call" | custom-call | flops 4529848320 | bytes 14532608 | tf_op jit(solution)/shard_map/mlp_block/pallas_call | solution.py:177
  349.7 9.1 %mlp_block.4 = bf16[432,512]{1,0:T(8,128)(2,1)S(1)} custom-call(s32[12]{0:T(128)S(1)} %stack.62.refs_0_, bf16[2,432,640]{2,1,0:T(8,128)(2,1)S(1)} %pad_maximum_fusion.refs_1_, bf16[2,432,640]{2,1,0:T(8,128)(2,1)S(1)} %copy-done.2, bf16[2,432,640]{2,1,0:T(8,128)(2,1)S(1)} %collective-permute-done.1.refs_3_, bf16[2,432,640]{2,1,0:T(8,128)(2,1)S(1)} %copy-done.5, ...), custom_call_target="tpu_custom_call" | custom-call | flops 4529848320 | bytes 14532608 | tf_op jit(solution)/shard_map/mlp_block/pallas_call | solution.py:177
  359.1 10.8 %collective-permute-done.19 = bf16[432,512]{1,0:T(8,128)(2,1)S(1)} collective-permute-done((bf16[432,512]{1,0:T(8,128)(2,1)S(1)}, bf16[432,512]{1,0:T(8,128)(2,1)S(1)}, u32[]{:S(2)}, u32[]{:S(2)}) %collective-permute-start.19) | collective-permute-done | bytes 442400 | tf_op jit(solution)/shard_map/ppermute | solution.py:215
  (104 shorter events, 37.8 us)
Async XLA Ops:
  17.5 91.7 %all-to-all-start = ((bf16[4,128,5120]{2,1,0:T(8,128)(2,1)}), bf16[4,128,5120]{2,1,0:T(8,128)(2,1)}, u32[]{:S(2)}, u32[]{:S(2)}) async-start(bf16[4,128,5120]{2,1,0:T(8,128)(2,1)} %bitcast.59), calls=%async_computation | async-start | bytes 10485760 | tf_op jit(solution)/shard_map/all_to_all | solution.py:279
  26.4 52.7 %collective-permute-start.1 = (bf16[2,432,640]{2,1,0:T(8,128)(2,1)S(1)}, bf16[2,432,640]{2,1,0:T(8,128)(2,1)S(1)}, u32[]{:S(2)}, u32[]{:S(2)}) collective-permute-start(bf16[2,432,640]{2,1,0:T(8,128)(2,1)S(1)} %pad_maximum_fusion.1), channel_id=1, source_target_pairs={{0,16},{4,20},{8,24},{12,28},{16,0},{20,4},{24,8},{28,12},{1,17},{... | collective-permute-start | bytes 3317768 | tf_op jit(solution)/shard_map/ppermute | solution.py:215
  79.1 28.4 %collective-permute-start.3 = (bf16[2,432,640]{2,1,0:T(8,128)(2,1)}, bf16[2,432,640]{2,1,0:T(8,128)(2,1)S(1)}, u32[]{:S(2)}, u32[]{:S(2)}) collective-permute-start(bf16[2,432,640]{2,1,0:T(8,128)(2,1)} %pad_maximum_fusion.2), channel_id=1, source_target_pairs={{0,8},{4,12},{8,16},{12,20},{16,24},{20,28},{24,0},{28,4},{1,9},{5... | collective-permute-start | bytes 3317768 | tf_op jit(solution)/shard_map/ppermute | solution.py:215
  133.3 31.1 %collective-permute-start.10 = (bf16[128,5120]{1,0:T(8,128)(2,1)}, bf16[128,5120]{1,0:T(8,128)(2,1)}, u32[]{:S(2)}, u32[]{:S(2)}) collective-permute-start(bf16[128,5120]{1,0:T(8,128)(2,1)} %multiply_convert_fusion.refs_9_), channel_id=1, source_target_pairs={{0,8},{4,12},{8,16},{12,20},{16,24},{20,28},{24,0},{28,4},{1,9},{5... | collective-permute-start | bytes 3932168 | tf_op jit(solution)/shard_map/ppermute | solution.py:215
  164.3 30.2 %collective-permute-start.15 = (bf16[128,5120]{1,0:T(8,128)(2,1)}, bf16[128,5120]{1,0:T(8,128)(2,1)}, u32[]{:S(2)}, u32[]{:S(2)}) collective-permute-start(bf16[128,5120]{1,0:T(8,128)(2,1)} %collective-permute-done.10.refs_9_), channel_id=1, source_target_pairs={{0,8},{4,12},{8,16},{12,20},{16,24},{20,28},{24,0},{28,4},{1,9},{5... | collective-permute-start | bytes 3932168 | tf_op jit(solution)/shard_map/ppermute | solution.py:215
  164.5 31.5 %collective-permute-start = (bf16[2,432,640]{2,1,0:T(8,128)(2,1)S(1)}, bf16[2,432,640]{2,1,0:T(8,128)(2,1)S(1)}, u32[]{:S(2)}, u32[]{:S(2)}) collective-permute-start(bf16[2,432,640]{2,1,0:T(8,128)(2,1)S(1)} %pad_maximum_fusion.refs_1_), channel_id=1, source_target_pairs={{0,4},{4,0},{8,12},{12,8},{16,20},{20,16},{24,28},{28,24},{1,5},{5... | collective-permute-start | bytes 3317768 | tf_op jit(solution)/shard_map/ppermute | solution.py:219
  166.1 49.5 %collective-permute-start.2 = (bf16[2,432,640]{2,1,0:T(8,128)(2,1)S(1)}, bf16[2,432,640]{2,1,0:T(8,128)(2,1)S(1)}, u32[]{:S(2)}, u32[]{:S(2)}) collective-permute-start(bf16[2,432,640]{2,1,0:T(8,128)(2,1)S(1)} %collective-permute-done.1.refs_3_), channel_id=1, source_target_pairs={{0,4},{4,0},{8,12},{12,8},{16,20},{20,16},{24,28},{28,24},{1,5},{5... | collective-permute-start | bytes 3317768 | tf_op jit(solution)/shard_map/ppermute | solution.py:219
  166.6 72.7 %collective-permute-start.4 = (bf16[2,432,640]{2,1,0:T(8,128)(2,1)S(1)}, bf16[2,432,640]{2,1,0:T(8,128)(2,1)S(1)}, u32[]{:S(2)}, u32[]{:S(2)}) collective-permute-start(bf16[2,432,640]{2,1,0:T(8,128)(2,1)S(1)} %collective-permute-done.3.refs_5_), channel_id=1, source_target_pairs={{0,4},{4,0},{8,12},{12,8},{16,20},{20,16},{24,28},{28,24},{1,5},{5... | collective-permute-start | bytes 3317768 | tf_op jit(solution)/shard_map/ppermute | solution.py:219
  194.5 74.8 %collective-permute-start.20 = (bf16[128,5120]{1,0:T(8,128)(2,1)}, bf16[128,5120]{1,0:T(8,128)(2,1)}, u32[]{:S(2)}, u32[]{:S(2)}) collective-permute-start(bf16[128,5120]{1,0:T(8,128)(2,1)} %collective-permute-done.15.refs_9_), channel_id=1, source_target_pairs={{0,8},{4,12},{8,16},{12,20},{16,24},{20,28},{24,0},{28,4},{1,9},{5... | collective-permute-start | bytes 3932168 | tf_op jit(solution)/shard_map/ppermute | solution.py:215
  194.5 74.7 %collective-permute-start.6 = (bf16[2,432,640]{2,1,0:T(8,128)(2,1)}, bf16[2,432,640]{2,1,0:T(8,128)(2,1)}, u32[]{:S(2)}, u32[]{:S(2)}) collective-permute-start(bf16[2,432,640]{2,1,0:T(8,128)(2,1)} %collective-permute-done.5.refs_7_), channel_id=1, source_target_pairs={{0,4},{4,0},{8,12},{12,8},{16,20},{20,16},{24,28},{28,24},{1,5},{5... | collective-permute-start | bytes 3317768 | tf_op jit(solution)/shard_map/ppermute | solution.py:219
  197.1 73.8 %collective-permute-start.7 = (bf16[128,5120]{1,0:T(8,128)(2,1)}, bf16[128,5120]{1,0:T(8,128)(2,1)}, u32[]{:S(2)}, u32[]{:S(2)}) collective-permute-start(bf16[128,5120]{1,0:T(8,128)(2,1)} %multiply_convert_fusion.refs_9_), channel_id=1, source_target_pairs={{0,2},{1,3},{2,0},{3,1},{4,6},{5,7},{6,4},{7,5},{8,10},{9,11},{10,... | collective-permute-start | bytes 3932168 | tf_op jit(solution)/shard_map/ppermute | solution.py:223
  216.6 54.5 %collective-permute-start.11 = (bf16[128,5120]{1,0:T(8,128)(2,1)}, bf16[128,5120]{1,0:T(8,128)(2,1)}, u32[]{:S(2)}, u32[]{:S(2)}) collective-permute-start(bf16[128,5120]{1,0:T(8,128)(2,1)} %collective-permute-done.10.refs_9_), channel_id=1, source_target_pairs={{0,2},{1,3},{2,0},{3,1},{4,6},{5,7},{6,4},{7,5},{8,10},{9,11},{10,... | collective-permute-start | bytes 3932168 | tf_op jit(solution)/shard_map/ppermute | solution.py:223
  240.3 45.0 %collective-permute-start.16 = (bf16[128,5120]{1,0:T(8,128)(2,1)}, bf16[128,5120]{1,0:T(8,128)(2,1)}, u32[]{:S(2)}, u32[]{:S(2)}) collective-permute-start(bf16[128,5120]{1,0:T(8,128)(2,1)} %collective-permute-done.15.refs_9_), channel_id=1, source_target_pairs={{0,2},{1,3},{2,0},{3,1},{4,6},{5,7},{6,4},{7,5},{8,10},{9,11},{10,... | collective-permute-start | bytes 3932168 | tf_op jit(solution)/shard_map/ppermute | solution.py:223
  241.9 68.1 %all-to-all-start.1 = ((bf16[8,128,512]{2,1,0:T(8,128)(2,1)}), bf16[8,128,512]{2,1,0:T(8,128)(2,1)}, u32[]{:S(2)}, u32[]{:S(2)}) async-start(bf16[8,128,512]{2,1,0:T(8,128)(2,1)} %bitcast.35), calls=%async_computation.1 | async-start | bytes 2097152 | tf_op jit(solution)/shard_map/all_to_all | solution.py:285
  269.3 39.2 %collective-permute-start.21 = (bf16[128,5120]{1,0:T(8,128)(2,1)}, bf16[128,5120]{1,0:T(8,128)(2,1)}, u32[]{:S(2)}, u32[]{:S(2)}) collective-permute-start(bf16[128,5120]{1,0:T(8,128)(2,1)} %collective-permute-done.20.refs_9_), channel_id=1, source_target_pairs={{0,2},{1,3},{2,0},{3,1},{4,6},{5,7},{6,4},{7,5},{8,10},{9,11},{10,... | collective-permute-start | bytes 3932168 | tf_op jit(solution)/shard_map/ppermute | solution.py:223
  270.9 37.7 %collective-permute-start.17 = (bf16[128,5120]{1,0:T(8,128)(2,1)}, bf16[128,5120]{1,0:T(8,128)(2,1)}, u32[]{:S(2)}, u32[]{:S(2)}) collective-permute-start(bf16[128,5120]{1,0:T(8,128)(2,1)} %collective-permute-done.15.refs_9_), channel_id=1, source_target_pairs={{0,1},{1,0},{2,3},{3,2},{4,5},{5,4},{6,7},{7,6},{8,9},{9,8},{10,11... | collective-permute-start | bytes 3932168 | tf_op jit(solution)/shard_map/ppermute | solution.py:227
  271.1 37.9 %collective-permute-start.13 = (bf16[128,5120]{1,0:T(8,128)(2,1)}, bf16[128,5120]{1,0:T(8,128)(2,1)}, u32[]{:S(2)}, u32[]{:S(2)}) collective-permute-start(bf16[128,5120]{1,0:T(8,128)(2,1)} %collective-permute-done.11.refs_10_), channel_id=1, source_target_pairs={{0,1},{1,0},{2,3},{3,2},{4,5},{5,4},{6,7},{7,6},{8,9},{9,8},{10,11... | collective-permute-start | bytes 3932168 | tf_op jit(solution)/shard_map/ppermute | solution.py:227
  285.3 41.7 %collective-permute-start.18 = (bf16[128,5120]{1,0:T(8,128)(2,1)}, bf16[128,5120]{1,0:T(8,128)(2,1)}, u32[]{:S(2)}, u32[]{:S(2)}) collective-permute-start(bf16[128,5120]{1,0:T(8,128)(2,1)} %collective-permute-done.16.refs_10_), channel_id=1, source_target_pairs={{0,1},{1,0},{2,3},{3,2},{4,5},{5,4},{6,7},{7,6},{8,9},{9,8},{10,11... | collective-permute-start | bytes 3932168 | tf_op jit(solution)/shard_map/ppermute | solution.py:227
  285.3 54.4 %collective-permute-start.22 = (bf16[128,5120]{1,0:T(8,128)(2,1)}, bf16[128,5120]{1,0:T(8,128)(2,1)}, u32[]{:S(2)}, u32[]{:S(2)}) collective-permute-start(bf16[128,5120]{1,0:T(8,128)(2,1)} %collective-permute-done.20.refs_9_), channel_id=1, source_target_pairs={{0,1},{1,0},{2,3},{3,2},{4,5},{5,4},{6,7},{7,6},{8,9},{9,8},{10,11... | collective-permute-start | bytes 3932168 | tf_op jit(solution)/shard_map/ppermute | solution.py:227
  308.5 31.3 %collective-permute-start.23 = (bf16[128,5120]{1,0:T(8,128)(2,1)}, bf16[128,5120]{1,0:T(8,128)(2,1)}, u32[]{:S(2)}, u32[]{:S(2)}) collective-permute-start(bf16[128,5120]{1,0:T(8,128)(2,1)} %collective-permute-done.21.refs_10_), channel_id=1, source_target_pairs={{0,1},{1,0},{2,3},{3,2},{4,5},{5,4},{6,7},{7,6},{8,9},{9,8},{10,11... | collective-permute-start | bytes 3932168 | tf_op jit(solution)/shard_map/ppermute | solution.py:227
  308.5 41.2 %collective-permute-start.8 = (bf16[128,5120]{1,0:T(8,128)(2,1)}, bf16[128,5120]{1,0:T(8,128)(2,1)}, u32[]{:S(2)}, u32[]{:S(2)}) collective-permute-start(bf16[128,5120]{1,0:T(8,128)(2,1)} %multiply_convert_fusion.refs_9_), channel_id=1, source_target_pairs={{0,1},{1,0},{2,3},{3,2},{4,5},{5,4},{6,7},{7,6},{8,9},{9,8},{10,11... | collective-permute-start | bytes 3932168 | tf_op jit(solution)/shard_map/ppermute | solution.py:227
  309.0 40.7 %collective-permute-start.9 = (bf16[128,5120]{1,0:T(8,128)(2,1)}, bf16[128,5120]{1,0:T(8,128)(2,1)}, u32[]{:S(2)}, u32[]{:S(2)}) collective-permute-start(bf16[128,5120]{1,0:T(8,128)(2,1)} %collective-permute-done.7.refs_10_), channel_id=1, source_target_pairs={{0,1},{1,0},{2,3},{3,2},{4,5},{5,4},{6,7},{7,6},{8,9},{9,8},{10,11... | collective-permute-start | bytes 3932168 | tf_op jit(solution)/shard_map/ppermute | solution.py:227
  327.0 32.0 %collective-permute-start.14 = (bf16[432,512]{1,0:T(8,128)(2,1)S(1)}, bf16[432,512]{1,0:T(8,128)(2,1)S(1)}, u32[]{:S(2)}, u32[]{:S(2)}) collective-permute-start(bf16[432,512]{1,0:T(8,128)(2,1)S(1)} %mlp_block.5), channel_id=1, source_target_pairs={{0,24},{4,28},{8,0},{12,4},{16,8},{20,12},{24,16},{28,20},{1,25},{... | collective-permute-start | bytes 1327112 | tf_op jit(solution)/shard_map/ppermute | solution.py:215
  339.7 30.1 %collective-permute-start.19 = (bf16[432,512]{1,0:T(8,128)(2,1)S(1)}, bf16[432,512]{1,0:T(8,128)(2,1)S(1)}, u32[]{:S(2)}, u32[]{:S(2)}) collective-permute-start(bf16[432,512]{1,0:T(8,128)(2,1)S(1)} %mlp_block.6), channel_id=1, source_target_pairs={{0,16},{4,20},{8,24},{12,28},{16,0},{20,4},{24,8},{28,12},{1,17},{... | collective-permute-start | bytes 1327112 | tf_op jit(solution)/shard_map/ppermute | solution.py:215
  (22 other events, 390.4 us)

commit v2 on v1

--- a/solution.py
+++ b/solution.py
@@ -11,6 +11,7 @@
 PAGE = 128
 REQS = 4
 CORES = 2
+N_Z = 4
 THETA = 1000000.0
 EPS = 1e-06
 NT = (((1,), (1,)), ((), ()))
@@ -25,7 +26,7 @@
     return jnp.concatenate([cosine, cosine], axis=-1), jnp.concatenate([-sine, sine], axis=-1)
 
 
-def attention_kernel(q_ref, k_ref, v_ref, qb_ref, kb_ref, vb_ref, cos_ref, sin_ref, segc_ref, segr_ref,
+def attention_kernel(order, q_ref, k_ref, v_ref, qb_ref, kb_ref, vb_ref, cos_ref, sin_ref, segc_ref, segr_ref,
                      slot_ref, out_ref, send_ref, q_buf, k_buf, v_buf, kv_buf):
     rows = q_ref.shape[0]
     kv_heads = k_ref.shape[1] // HD
@@ -78,17 +79,21 @@
             weights = jnp.where(allowed, jnp.exp(scores - row_max), 0.0)
             total = jnp.sum(weights, axis=-1, keepdims=True)
             probs = (weights / jnp.where(total > 0.0, total, 1.0)).astype(jnp.bfloat16)
-            out_ref[start:high, head * HD:(head + 1) * HD] = jnp.dot(
+            mixed = jnp.dot(
                 probs, v_buf[low:high, kv_cols], preferred_element_type=jnp.float32
             ).astype(jnp.bfloat16)
-
-
-def attention(q_pre, k_pre, v_pre, q_bias, k_bias, v_bias, cosine, sine, segs, slots, slot_count):
+            size = rows // len(order)
+            for at in range(0, tile, size):
+                to = order[(start + at) // size] * size
+                out_ref[to:to + size, head * HD:(head + 1) * HD] = mixed[at:at + size]
+
+
+def attention(q_pre, k_pre, v_pre, q_bias, k_bias, v_bias, cosine, sine, segs, slots, slot_count, order):
     rows, q_cols = q_pre.shape
     kv_cols = k_pre.shape[1]
     vmem = pl.BlockSpec(memory_space=pltpu.VMEM)
     return pl.pallas_call(
-        attention_kernel,
+        lambda *refs: attention_kernel(order, *refs),
         out_shape=(
             jax.ShapeDtypeStruct((rows, q_cols), jnp.bfloat16),
             jax.ShapeDtypeStruct((slot_count, 2 * kv_cols), jnp.bfloat16),
@@ -102,7 +107,7 @@
             pltpu.VMEM((rows, 2 * kv_cols), jnp.bfloat16),
         ],
         compiler_params=pltpu.CompilerParams(vmem_limit_bytes=32 * 2**20),
-        cost_estimate=pl.CostEstimate(flops=2 * 10**9, bytes_accessed=4 * 2**20, transcendentals=10**6),
+        cost_estimate=pl.CostEstimate(flops=3 * 10**10, bytes_accessed=4 * 2**20, transcendentals=10**6),
         name="attention",
     )(q_pre, k_pre, v_pre, q_bias[None], k_bias[None], v_bias[None], cosine, sine, segs[:, None], segs[None],
       slots[None])
@@ -127,16 +132,23 @@
     )(sources, pages_in)
 
 
-def mlp_kernel(count, pieces, ids_ref, *refs):
+def mlp_kernel(count, pieces, halves, ids_ref, *refs):
     weights = refs[:count]
     rows_in = refs[count:count + pieces]
     out_ref, gate_buf, up_buf, row_buf, weight_sems, row_sems = refs[count + pieces:]
     depth = weights[0].shape[2]
-    piece = rows_in[0].shape[0]
+    piece = rows_in[0].shape[0] // halves
     copies = []
     for index in range(pieces):
-        at = pl.multiple_of(ids_ref[count + index] * piece, piece)
-        copies.append(pltpu.make_async_copy(rows_in[index], row_buf.at[pl.ds(at, piece), :], row_sems.at[index]))
+        for half in range(halves):
+            at = pl.multiple_of((half * pieces + ids_ref[count + index]) * piece, piece)
+            copies.append(
+                pltpu.make_async_copy(
+                    rows_in[index].at[pl.ds(half * piece, piece), :],
+                    row_buf.at[pl.ds(at, piece), :],
+                    row_sems.at[index, half],
+                )
+            )
     for index in range(count):
         at = pl.multiple_of(ids_ref[index] * depth, depth)
         for which, buf in enumerate((gate_buf, up_buf)):
@@ -157,25 +169,28 @@
         out_ref[:, start:start + tile] = (gate / (1.0 + jnp.exp(-gate)) * up).astype(jnp.bfloat16)
 
 
-def mlp_block(weights, weight_ids, rows_in, row_ids):
+def mlp_block(weights, weight_ids, rows_in, row_ids, halves):
     count, pieces = len(weights), len(rows_in)
     units, depth = weights[0].shape[1:]
-    piece, width = rows_in[0].shape
-    tokens = piece * pieces
+    width = rows_in[0].shape[1]
+    piece = rows_in[0].shape[0] // halves
+    tokens = piece * pieces * halves
     if depth % 128 or units % 16 or piece % 16:
         both = jnp.zeros((2, units, width), jnp.bfloat16)
         for index in range(count):
             both = lax.dynamic_update_slice(both, weights[index], (0, 0, weight_ids[index] * depth))
         rows = jnp.zeros((tokens, width), jnp.bfloat16)
         for index in range(pieces):
-            rows = lax.dynamic_update_slice(rows, rows_in[index], (row_ids[index] * piece, 0))
+            for half in range(halves):
+                at = (half * pieces + row_ids[index]) * piece
+                rows = lax.dynamic_update_slice(rows, rows_in[index][half * piece:(half + 1) * piece], (at, 0))
         gate = lax.dot_general(both[0], rows, NT, preferred_element_type=jnp.float32)
         up = lax.dot_general(both[1], rows, NT, preferred_element_type=jnp.float32)
         return (jax.nn.silu(gate) * up).astype(jnp.bfloat16)
     ids = jnp.stack([jnp.asarray(i, jnp.int32) for i in list(weight_ids) + list(row_ids)])
     anywhere = pl.BlockSpec(memory_space=pl.ANY)
     return pl.pallas_call(
-        lambda *refs: mlp_kernel(count, pieces, *refs),
+        lambda *refs: mlp_kernel(count, pieces, halves, *refs),
         out_shape=jax.ShapeDtypeStruct((units, tokens), jnp.bfloat16),
         in_specs=[pl.BlockSpec(memory_space=pltpu.SMEM)] + [anywhere] * (count + pieces),
         out_specs=pl.BlockSpec(memory_space=pltpu.VMEM),
@@ -184,9 +199,9 @@
             pltpu.VMEM((units, width), jnp.bfloat16),
             pltpu.VMEM((tokens, width), jnp.bfloat16),
             pltpu.SemaphoreType.DMA((2, count)),
-            pltpu.SemaphoreType.DMA((pieces,)),
+            pltpu.SemaphoreType.DMA((pieces, halves)),
         ],
-        compiler_params=pltpu.CompilerParams(vmem_limit_bytes=48 * 2**20),
+        compiler_params=pltpu.CompilerParams(vmem_limit_bytes=32 * 2**20),
         cost_estimate=pl.CostEstimate(
             flops=4 * units * width * tokens,
             bytes_accessed=2 * (2 * units * width + tokens * width + units * tokens),
@@ -196,65 +211,75 @@
     )(ids, *weights, *rows_in)
 
 
+def after(value, *before):
+    return lax.optimization_barrier((value,) + before)[0]
+
+
 def shards(q_pre, k_pre, v_pre, q_bias, k_bias, v_bias, segment_ids, lengths, page_table, w_out, residual,
            norm_gain, w_gate, w_up):
     me_req = lax.axis_index("req")
     me_mp = lax.axis_index("mp")
     n_req = lax.axis_size("req")
     n_mp = lax.axis_size("mp")
-    n_z = 4 if n_req % 4 == 0 else 1
-    n_y = n_req // n_z
+    n_y = n_req // N_Z
     n_x = n_mp // CORES
     z = me_req // n_y
     y = me_req % n_y
     x = me_mp // CORES
     core = me_mp % CORES
 
-    def along_z(value, shift):
-        pairs = [(a * n_y + b, (a + shift) % n_z * n_y + b) for a in range(n_z) for b in range(n_y)]
-        return lax.ppermute(value, "req", pairs)
-
-    def along_y(value, shift):
-        pairs = [(a * n_y + b, a * n_y + (b + shift) % n_y) for a in range(n_z) for b in range(n_y)]
-        return lax.ppermute(value, "req", pairs)
-
-    def along_x(value, shift):
-        pairs = [(a * CORES + b, (a + shift) % n_x * CORES + b) for a in range(n_x) for b in range(CORES)]
-        return lax.ppermute(value, "mp", pairs)
+    def along_z(value, moves):
+        return lax.ppermute(value, "req", [(a * n_y + c, b * n_y + c) for a, b in moves for c in range(n_y)])
+
+    def turn_z(value, shift):
+        return along_z(value, [(a, (a + shift) % N_Z) for a in range(N_Z)])
+
+    def along_y(value):
+        return [
+            lax.ppermute(
+                value, "req", [(a * n_y + b, a * n_y + (b + step) % n_y) for a in range(N_Z) for b in range(n_y)]
+            )
+            for step in range(1, n_y)
+        ]
+
+    def along_x(value):
+        return [
+            lax.ppermute(
+                value,
+                "mp",
+                [(a * CORES + b, (a + step) % n_x * CORES + b) for a in range(n_x) for b in range(CORES)],
+            )
+            for step in range(1, n_x)
+        ]
 
     def across_cores(value):
-        pairs = [(a * CORES + b, a * CORES + 1 - b) for a in range(n_x) for b in range(CORES)]
-        return lax.ppermute(value, "mp", pairs)
+        return lax.ppermute(
+            value, "mp", [(a * CORES + b, a * CORES + 1 - b) for a in range(n_x) for b in range(CORES)]
+        )
 
     units_all, depth = w_gate.shape[1], w_gate.shape[0]
-    units = units_all // n_z
-    gate_t, up_t = w_gate.T, w_up.T
-
-    def share(target):
+    units = units_all // N_Z
+
+    def share(gate_t, up_t, target):
         at = (target * units, 0)
         return jnp.stack(
             [lax.dynamic_slice(gate_t, at, (units, depth)), lax.dynamic_slice(up_t, at, (units, depth))]
         )
 
-    weights, weight_ids = [], []
-
-    def arrived(chunk, shift):
-        source_z = (z - shift) % n_z
-        weights.append(chunk)
-        weight_ids.append(source_z * n_y + y)
-        for step in range(1, n_y):
-            weights.append(along_y(chunk, step))
-            weight_ids.append(source_z * n_y + (y - step) % n_y)
-
-    arrived(share(z), 0)
-    last = None
-    shifts = [n_z // 2] + [s for s in range(1, n_z) if s != n_z // 2]
-    for shift in shifts if n_z > 1 else []:
-        chunk = share((z + shift) % n_z)
-        if last is not None:
-            chunk, last = lax.optimization_barrier((chunk, last))
-        last = along_z(chunk, shift)
-        arrived(last, shift)
+    def source_ids(shift):
+        source_z = (z - shift) % N_Z
+        return [source_z * n_y + (y - step) % n_y for step in range(n_y)]
+
+    gate_t, up_t = w_gate.T, w_up.T
+    first = share(gate_t, up_t, (z + 2) % N_Z)
+    gate_t, up_t, first, q_pre, segment_ids = lax.optimization_barrier((gate_t, up_t, first, q_pre, segment_ids))
+    own = share(gate_t, up_t, z)
+    from_2 = turn_z(first, 2)
+    own_y = along_y(own)
+    from_1 = turn_z(after(share(gate_t, up_t, (z + 1) % N_Z), from_2, *own_y), 1)
+    from_2_y = along_y(from_2)
+    from_3 = turn_z(after(share(gate_t, up_t, (z + 3) % N_Z), from_1, *from_2_y), 3)
+    from_1_y = along_y(from_1)
 
     rows = q_pre.shape[0]
     kv_heads = k_pre.shape[1] // HD
@@ -270,17 +295,74 @@
     row_pos = jnp.arange(rows, dtype=jnp.int32) - row_start
     slots = jnp.where(alive, row_owner * PAGE + row_pos, -1)
     cosine, sine = rope_tables(row_pos.astype(jnp.float32))
+    order = [group % n_mp * 2 + group // n_mp for group in range(2 * n_mp)]
     attended, kv_send = attention(
-        q_pre, k_pre, v_pre, q_bias, k_bias, v_bias, cosine, sine, segment_ids, slots, n_req * PAGE
+        q_pre, k_pre, v_pre, q_bias, k_bias, v_bias, cosine, sine, segment_ids, slots, n_req * PAGE, order
     )
     partial = jnp.dot(attended, w_out, preferred_element_type=jnp.float32).astype(jnp.bfloat16)
     width = partial.shape[1]
-    piece = rows // n_mp
-    parts = lax.all_to_all(partial.reshape(n_mp, piece, width), "mp", split_axis=0, concat_axis=0, tiled=True)
+    run = rows // n_mp // 2
+    parts = lax.all_to_all(partial.reshape(n_mp, 2 * run, width), "mp", split_axis=0, concat_axis=0, tiled=True)
     summed = jnp.sum(parts.astype(jnp.float32), axis=0)
-    state = lax.dynamic_slice(residual, (me_mp * piece, 0), (piece, width)).astype(jnp.float32) + summed
+    residual_rows = jnp.concatenate(
+        [
+            lax.dynamic_slice(residual, (me_mp * run, 0), (run, width)),
+            lax.dynamic_slice(residual, (rows // 2 + me_mp * run, 0), (run, width)),
+        ]
+    )
+    state = residual_rows.astype(jnp.float32) + summed
     scale = lax.rsqrt(jnp.mean(state * state, axis=-1, keepdims=True) + EPS)
     normed = (state * scale * norm_gain).astype(jnp.bfloat16)
+
+    row_ids = [(x - step) % n_x * CORES + core for step in range(n_x)]
+    row_ids += [(x - step) % n_x * CORES + 1 - core for step in range(n_x)]
+    normed_x = along_x(normed)
+    normed = after(normed, from_3, *from_1_y)
+    from_3_y = along_y(from_3)
+    up_1 = along_z(normed, [(0, 1), (1, 2), (2, 3)])
+    down_1 = along_z(normed, [(1, 0), (2, 1), (3, 2)])
+    up_1, down_1, *_ = lax.optimization_barrier((up_1, down_1, *from_3_y, *normed_x))
+    up_2 = along_z(up_1, [(1, 2), (2, 3)])
+    down_2 = along_z(down_1, [(1, 0), (2, 1)])
+    block_1 = jnp.where(z % 2 == 0, down_1, up_1)
+    block_1_x = along_x(block_1)
+    up_2, down_2, *_ = lax.optimization_barrier((up_2, down_2, *block_1_x))
+    up_3a = along_z(up_2[:run], [(2, 3)])
+    down_3a = along_z(down_2[:run], [(1, 0)])
+    block_2 = jnp.where(z < 2, down_2, up_2)
+    block_2_x = along_x(block_2)
+    kv_send = after(kv_send, up_2, down_2)
+    up_3a, down_3a = lax.optimization_barrier((up_3a, down_3a))
+    up_3b = along_z(after(up_2[run:], up_3a, down_3a), [(2, 3)])
+    down_3b = along_z(after(down_2[run:], up_3a, down_3a), [(1, 0)])
+
+    def last_block(half, up, down):
+        at = slice(half * run, (half + 1) * run)
+        return jnp.where(z == 0, down, jnp.where(z == 3, up, jnp.where(z == 1, down_1[at], up_1[at])))
+
+    block_3a = after(last_block(0, up_3a, down_3a), *block_2_x)
+    block_3b = last_block(1, up_3b, down_3b)
+    block_3a_x = along_x(block_3a)
+    block_3b_x = along_x(after(block_3b, *block_3a_x))
+
+    weights = [own, *own_y, from_2, *from_2_y, from_1, *from_1_y, from_3, *from_3_y]
+    weight_ids = [i for shift in (0, 2, 1, 3) for i in source_ids(shift)]
+
+    def work(block, block_x, halves):
+        pieces = [block, *block_x]
+        return mlp_block(weights, weight_ids, pieces + [across_cores(p) for p in pieces], row_ids, halves)
+
+    hidden_t = jnp.zeros((units_all, rows), jnp.bfloat16)
+    hidden_t = lax.dynamic_update_slice(hidden_t, work(normed, normed_x, 2), (z * units, 0))
+    for flip, half, block, block_x in (
+        (1, 0, block_1, block_1_x),
+        (2, 0, block_2, block_2_x),
+        (3, 0, block_3a, block_3a_x),
+        (3, 1, block_3b, block_3b_x),
+    ):
+        done = work(block, block_x, block.shape[0] // run)
+        done = along_z(done, [(a, a ^ flip) for a in range(N_Z)])
+        hidden_t = lax.dynamic_update_slice(hidden_t, done, ((z ^ flip) * units, half * (rows // 2)))
 
     kv_in = lax.all_to_all(
         kv_send.reshape(n_req, PAGE, 2 * kv_heads * HD), "req", split_axis=0, concat_axis=0, tiled=True
@@ -288,24 +370,6 @@
     mine = page_table[None] == (me_req * REQS + jnp.arange(REQS, dtype=jnp.int32))[:, None, None]
     sources = jnp.sum(jnp.where(mine, jnp.arange(n_req, dtype=jnp.int32)[None, :, None], 0), axis=(1, 2))
     cache_out = write_cache(sources.astype(jnp.int32), kv_in, kv_heads)
-
-    def spread(own):
-        across = [(own, x)] + [(along_x(own, step), (x - step) % n_x) for step in range(1, n_x)]
-        pieces = [(value, at * CORES + core) for value, at in across]
-        pieces += [(across_cores(value), at * CORES + 1 - core) for value, at in across]
-        return [p[0] for p in pieces], [p[1] for p in pieces]
-
-    normed, last = lax.optimization_barrier((normed, last)) if last is not None else (normed, None)
-    hidden_t = jnp.zeros((units_all, rows), jnp.bfloat16)
-    block = normed
-    for step in range(n_z):
-        if step:
-            block = along_z(block, 1)
-        values, at = spread(block)
-        done = mlp_block(weights, weight_ids, values, at)
-        if step:
-            done = along_z(done, -step)
-        hidden_t = lax.dynamic_update_slice(hidden_t, done, ((z + step) % n_z * units, 0))
     return hidden_t.T, cache_out
 
 

time: 372 us -> 356 us (0.957); the launches traced: 371 us -> 350 us
  waiting for transfers between devices: 254 us -> 199 us
  starting transfers between devices: 35.3 us -> 48.2 us
  local copies, waits for them, and re-layouts: 13.2 us -> 21.1 us
  Pallas kernels: 46.3 us -> 52.8 us
  other arithmetic: 15.5 us -> 22 us
    ppermute x25 -> x34, waiting for transfers between devices: 254 us -> 199 us  [the longest x4 80.4 us: along_y(): lax.ppermute(value, 'req', [(a * n_y + b, a * n_y + (b + step) % n_y) for...]
    ppermute x25 -> x34, starting transfers between devices: 24.2 us -> 38.2 us  [the longest x15 25.7 us: along_z(): lax.ppermute(value, 'req', [(a * n_y + c, b * n_y + c) for a, b in moves...]
    select_n x0 -> x3, other arithmetic: none -> 8.49 us  [the longest x1 3.4 us: last_block(): jnp.where(z == 0, down, jnp.where(z == 3, up, jnp.where(z == 1, down_1[at...]
    pallas_call x5 -> x6, Pallas kernels: 40.8 us -> 47.4 us  [the longest x5 42.8 us: mlp_block(): pl.pallas_call(lambda *refs: mlp_kernel(count, pieces, halves, *refs), ou...]
    dynamic_update_slice x4 -> x5, local copies, waits for them, and re-layouts: 0.14 us -> 4.78 us  [the longest x4 3.99 us: shards(): lax.dynamic_update_slice(hidden_t, done, ((z ^ flip) * units, half * (row...]
  transfers between devices with their start and end apart: 27 -> 36, of which waited for: 11 -> 14; matrix products, arithmetic and copies ran while one was open for 4% -> 7% of each run, Pallas kernels for 11% -> 14%
where the time goes in v2:
time: 356 us; the launch traced here: 350 us
  waiting for transfers between devices  199 us (56%)
  Pallas kernels  52.8 us (15%)
  starting transfers between devices  48.2 us (14%)
  other arithmetic  22 us (6%)
  local copies, waits for them, and re-layouts  21.1 us (6%)
  matrix products  6.1 us (2%)
    ppermute x4, waiting for transfers between devices, along_y(): lax.ppermute(value, 'req', [(a * n_y + b, a * n_y + (b + step) % n_y) for...  80.4 us
    ppermute x15, waiting for transfers between devices, along_z(): lax.ppermute(value, 'req', [(a * n_y + c, b * n_y + c) for a, b in moves...  68.4 us
    ppermute x5, waiting for transfers between devices, along_x(): lax.ppermute(value, 'mp', [(a * CORES + b, (a + step) % n_x * CORES + b)...  49.9 us
    pallas_call x5, Pallas kernels, mlp_block(): pl.pallas_call(lambda *refs: mlp_kernel(count, pieces, halves, *refs), ou...  42.8 us
    ppermute x15, starting transfers between devices, along_z(): lax.ppermute(value, 'req', [(a * n_y + c, b * n_y + c) for a, b in moves...  25.7 us
  transfers between devices with their start and end apart: 36, of which 14 were waited for; matrix products, arithmetic and copies ran while one was open for 7% of the time, Pallas kernels for 14%

profile of v2, /device:TPU:0, one launch (start us, length us, event | category | flops | bytes accessed | tf_op | source)
XLA Modules:
  0.0 350.0 jit_solution(17218642767061235665)
XLA Ops:
  8.5 4.5 %attention.1 = (bf16[512,768]{1,0:T(8,128)(2,1)S(1)}, bf16[1024,512]{1,0:T(8,128)(2,1)S(1)}) custom-call(bf16[512,768]{1,0:T(8,128)(2,1)S(1)} %copy-done.6, bf16[512,256]{1,0:T(8,128)(2,1)S(1)} %copy-done.7, bf16[512,256]{1,0:T(8,128)(2,1)S(1)} %copy-done.8, f32[1,768]{1,0:T(1,128)S(1)} %broadcast_in_dim.71.refs_3_, f32[1,256]{1,0:T(1,128)S(1)} %bitcast.48, ...), custom_call_target="tpu_custom_call" | custom-call | flops 30000001024 | bytes 4194304 | tf_op jit(solution)/shard_map/attention/pallas_call | solution.py:95
  13.0 6.1 %convolution_convert_fusion = bf16[512,5120]{1,0:T(8,128)(2,1)} fusion(bf16[512,768]{1,0:T(8,128)(2,1)S(1)} %get-tuple-element.30, bf16[768,5120]{1,0:T(8,128)(2,1)S(1)} %copy-done.22), kind=kOutput, calls=%fused_computation.1 | convolution fusion | flops 4029153280 | bytes 13893632 | tf_op jit(solution)/shard_map/dot_general | solution.py:302
  19.1 5.2 %all-to-all-start = ((bf16[4,128,5120]{2,1,0:T(8,128)(2,1)}), bf16[4,128,5120]{2,1,0:T(8,128)(2,1)}, u32[]{:S(2)}, u32[]{:S(2)}) async-start(bf16[4,128,5120]{2,1,0:T(8,128)(2,1)} %bitcast.50), calls=%async_computation | async-start | bytes 10485760 | tf_op jit(solution)/shard_map/all_to_all | solution.py:305
  34.2 21.2 %collective-permute-done.refs_2_ = bf16[2,432,640]{2,1,0:T(8,128)(2,1)S(1)} collective-permute-done((bf16[2,432,640]{2,1,0:T(8,128)(2,1)S(1)}, bf16[2,432,640]{2,1,0:T(8,128)(2,1)S(1)}, u32[]{:S(2)}, u32[]{:S(2)}) %collective-permute-start) | collective-permute-done | bytes 1105952 | tf_op jit(solution)/shard_map/ppermute | solution.py:239
  55.4 26.1 %collective-permute-done.1.refs_3_ = bf16[2,432,640]{2,1,0:T(8,128)(2,1)S(1)} collective-permute-done((bf16[2,432,640]{2,1,0:T(8,128)(2,1)S(1)}, bf16[2,432,640]{2,1,0:T(8,128)(2,1)S(1)}, u32[]{:S(2)}, u32[]{:S(2)}) %collective-permute-start.1) | collective-permute-done | bytes 1105952 | tf_op jit(solution)/shard_map/ppermute | solution.py:232
  88.3 19.0 %collective-permute-done.2.refs_4_ = bf16[2,432,640]{2,1,0:T(8,128)(2,1)} collective-permute-done((bf16[2,432,640]{2,1,0:T(8,128)(2,1)S(1)}, bf16[2,432,640]{2,1,0:T(8,128)(2,1)}, u32[]{:S(2)}, u32[]{:S(2)}) %collective-permute-start.2) | collective-permute-done | bytes 1105952 | tf_op jit(solution)/shard_map/ppermute | solution.py:239
  113.4 3.8 %convert_reduce_fusion = f32[128,5120]{1,0:T(8,128)S(1)} fusion(bf16[4,128,5120]{2,1,0:T(8,128)(2,1)} %all-to-all-done), kind=kLoop, calls=%fused_computation | loop fusion | flops 4587520 | bytes 7864320 | tf_op jit(solution)/shard_map/reduce_sum | solution.py:306
  121.1 16.9 %collective-permute-done.4.refs_6_ = bf16[2,432,640]{2,1,0:T(8,128)(2,1)} collective-permute-done((bf16[2,432,640]{2,1,0:T(8,128)(2,1)}, bf16[2,432,640]{2,1,0:T(8,128)(2,1)}, u32[]{:S(2)}, u32[]{:S(2)}) %collective-permute-start.4) | collective-permute-done | bytes 1105952 | tf_op jit(solution)/shard_map/ppermute | solution.py:239
  143.1 23.3 %collective-permute-done.6.refs_8_ = bf16[2,432,640]{2,1,0:T(8,128)(2,1)} collective-permute-done((bf16[2,432,640]{2,1,0:T(8,128)(2,1)}, bf16[2,432,640]{2,1,0:T(8,128)(2,1)}, u32[]{:S(2)}, u32[]{:S(2)}) %collective-permute-start.6) | collective-permute-done | bytes 1105952 | tf_op jit(solution)/shard_map/ppermute | solution.py:239
  166.5 4.9 %collective-permute-done.11 = bf16[128,5120]{1,0:T(8,128)(2,1)} collective-permute-done((bf16[128,5120]{1,0:T(8,128)(2,1)}, bf16[128,5120]{1,0:T(8,128)(2,1)}, u32[]{:S(2)}, u32[]{:S(2)}) %collective-permute-start.11) | collective-permute-done | bytes 1310752 | tf_op jit(solution)/shard_map/ppermute | solution.py:232
  177.7 23.7 %collective-permute-done.12.refs_10_ = bf16[128,5120]{1,0:T(8,128)(2,1)} collective-permute-done((bf16[128,5120]{1,0:T(8,128)(2,1)}, bf16[128,5120]{1,0:T(8,128)(2,1)}, u32[]{:S(2)}, u32[]{:S(2)}) %collective-permute-start.12) | collective-permute-done | bytes 1310752 | tf_op jit(solution)/shard_map/ppermute | solution.py:247
  201.4 5.6 %collective-permute-done.17 = bf16[128,5120]{1,0:T(8,128)(2,1)S(1)} collective-permute-done((bf16[128,5120]{1,0:T(8,128)(2,1)}, bf16[128,5120]{1,0:T(8,128)(2,1)S(1)}, u32[]{:S(2)}, u32[]{:S(2)}) %collective-permute-start.17) | collective-permute-done | bytes 1310752 | tf_op jit(solution)/shard_map/ppermute | solution.py:232
  212.4 13.6 %collective-permute-done.23 = bf16[64,5120]{1,0:T(8,128)(2,1)} collective-permute-done((bf16[64,5120]{1,0:T(8,128)(2,1)}, bf16[64,5120]{1,0:T(8,128)(2,1)}, u32[]{:S(2)}, u32[]{:S(2)}) %collective-permute-start.23) | collective-permute-done | bytes 655392 | tf_op jit(solution)/shard_map/ppermute | solution.py:232
  232.5 7.1 %collective-permute-done.28 = bf16[64,5120]{1,0:T(8,128)(2,1)} collective-permute-done((bf16[64,5120]{1,0:T(8,128)(2,1)}, bf16[64,5120]{1,0:T(8,128)(2,1)}, u32[]{:S(2)}, u32[]{:S(2)}) %collective-permute-start.28) | collective-permute-done | bytes 655392 | tf_op jit(solution)/shard_map/ppermute | solution.py:232
  243.0 17.4 %collective-permute-done.18.refs_10_ = bf16[128,5120]{1,0:T(8,128)(2,1)} collective-permute-done((bf16[128,5120]{1,0:T(8,128)(2,1)}, bf16[128,5120]{1,0:T(8,128)(2,1)}, u32[]{:S(2)}, u32[]{:S(2)}) %collective-permute-start.18) | collective-permute-done | bytes 1310752 | tf_op jit(solution)/shard_map/ppermute | solution.py:247
  262.5 8.8 %collective-permute-done.24.refs_10_ = bf16[64,5120]{1,0:T(8,128)(2,1)} collective-permute-done((bf16[64,5120]{1,0:T(8,128)(2,1)}, bf16[64,5120]{1,0:T(8,128)(2,1)}, u32[]{:S(2)}, u32[]{:S(2)}) %collective-permute-start.24) | collective-permute-done | bytes 655392 | tf_op jit(solution)/shard_map/ppermute | solution.py:247
  271.3 4.8 %all-to-all-start.1 = ((bf16[8,128,512]{2,1,0:T(8,128)(2,1)}), bf16[8,128,512]{2,1,0:T(8,128)(2,1)}, u32[]{:S(2)}, u32[]{:S(2)}) async-start(bf16[8,128,512]{2,1,0:T(8,128)(2,1)} %bitcast.44), calls=%async_computation.1 | async-start | bytes 2097152 | tf_op jit(solution)/shard_map/all_to_all | solution.py:367
  278.7 9.4 %mlp_block.5 = bf16[432,512]{1,0:T(8,128)(2,1)S(1)} custom-call(s32[12]{0:T(128)S(1)} %stack.62.refs_0_, bf16[2,432,640]{2,1,0:T(8,128)(2,1)S(1)} %pad_maximum_fusion.2.refs_1_, bf16[2,432,640]{2,1,0:T(8,128)(2,1)S(1)} %collective-permute-done.refs_2_, bf16[2,432,640]{2,1,0:T(8,128)(2,1)S(1)} %collective-permute-done.1.refs_3_, ...), custom_call_target="tpu_custom_call" | custom-call | flops 4529848320 | bytes 14532608 | tf_op jit(solution)/shard_map/mlp_block/pallas_call | solution.py:192
  288.1 9.7 %mlp_block.6 = bf16[432,512]{1,0:T(8,128)(2,1)S(1)} custom-call(s32[12]{0:T(128)S(1)} %stack.62.refs_0_, bf16[2,432,640]{2,1,0:T(8,128)(2,1)S(1)} %pad_maximum_fusion.2.refs_1_, bf16[2,432,640]{2,1,0:T(8,128)(2,1)S(1)} %collective-permute-done.refs_2_, bf16[2,432,640]{2,1,0:T(8,128)(2,1)S(1)} %collective-permute-done.1.refs_3_, ...), custom_call_target="tpu_custom_call" | custom-call | flops 4529848320 | bytes 14532608 | tf_op jit(solution)/shard_map/mlp_block/pallas_call | solution.py:192
  304.2 10.5 %mlp_block.7 = bf16[432,512]{1,0:T(8,128)(2,1)} custom-call(s32[12]{0:T(128)S(1)} %stack.62.refs_0_, bf16[2,432,640]{2,1,0:T(8,128)(2,1)S(1)} %pad_maximum_fusion.2.refs_1_, bf16[2,432,640]{2,1,0:T(8,128)(2,1)S(1)} %collective-permute-done.refs_2_, bf16[2,432,640]{2,1,0:T(8,128)(2,1)S(1)} %collective-permute-done.1.refs_3_, ...), custom_call_target="tpu_custom_call" | custom-call | flops 4529848320 | bytes 14532608 | tf_op jit(solution)/shard_map/mlp_block/pallas_call | solution.py:192
  316.8 5.4 %write_cache.1 = bf16[4,2,128,256]{3,2,1,0:T(8,128)(2,1)} custom-call(s32[4]{0:T(128)} %select_reduce_fusion.source_ref, bf16[8,128,512]{2,1,0:T(8,128)(2,1)} %all-to-all-done.1.in_ref), custom_call_target="tpu_custom_call" | custom-call | tf_op jit(solution)/shard_map/write_cache/pallas_call | solution.py:127
  322.2 6.6 %mlp_block.8 = bf16[432,256]{1,0:T(8,128)(2,1)S(1)} custom-call(s32[12]{0:T(128)S(1)} %stack.62.refs_0_, bf16[2,432,640]{2,1,0:T(8,128)(2,1)S(1)} %pad_maximum_fusion.2.refs_1_, bf16[2,432,640]{2,1,0:T(8,128)(2,1)S(1)} %collective-permute-done.refs_2_, bf16[2,432,640]{2,1,0:T(8,128)(2,1)S(1)} %collective-permute-done.1.refs_3_, ...), custom_call_target="tpu_custom_call" | custom-call | flops 2264924160 | bytes 11689984 | tf_op jit(solution)/shard_map/mlp_block/pallas_call | solution.py:192
  330.1 6.6 %mlp_block.9 = bf16[432,256]{1,0:T(8,128)(2,1)S(1)} custom-call(s32[12]{0:T(128)S(1)} %stack.62.refs_0_, bf16[2,432,640]{2,1,0:T(8,128)(2,1)S(1)} %pad_maximum_fusion.2.refs_1_, bf16[2,432,640]{2,1,0:T(8,128)(2,1)S(1)} %collective-permute-done.refs_2_, bf16[2,432,640]{2,1,0:T(8,128)(2,1)S(1)} %collective-permute-done.1.refs_3_, ...), custom_call_target="tpu_custom_call" | custom-call | flops 2264924160 | bytes 11689984 | tf_op jit(solution)/shard_map/mlp_block/pallas_call | solution.py:192
  339.5 7.3 %collective-permute-done.21 = bf16[432,512]{1,0:T(8,128)(2,1)} collective-permute-done((bf16[432,512]{1,0:T(8,128)(2,1)}, bf16[432,512]{1,0:T(8,128)(2,1)}, u32[]{:S(2)}, u32[]{:S(2)}) %collective-permute-start.21) | collective-permute-done | bytes 442400 | tf_op jit(solution)/shard_map/ppermute | solution.py:232
  (140 shorter events, 81.2 us)
Async XLA Ops:
  19.1 94.3 %all-to-all-start = ((bf16[4,128,5120]{2,1,0:T(8,128)(2,1)}), bf16[4,128,5120]{2,1,0:T(8,128)(2,1)}, u32[]{:S(2)}, u32[]{:S(2)}) async-start(bf16[4,128,5120]{2,1,0:T(8,128)(2,1)} %bitcast.50), calls=%async_computation | async-start | bytes 10485760 | tf_op jit(solution)/shard_map/all_to_all | solution.py:305
  27.4 28.0 %collective-permute-start = (bf16[2,432,640]{2,1,0:T(8,128)(2,1)S(1)}, bf16[2,432,640]{2,1,0:T(8,128)(2,1)S(1)}, u32[]{:S(2)}, u32[]{:S(2)}) collective-permute-start(bf16[2,432,640]{2,1,0:T(8,128)(2,1)S(1)} %pad_maximum_fusion.2.refs_1_), channel_id=1, source_target_pairs={{0,4},{4,0},{8,12},{12,8},{16,20},{20,16},{24,28},{28,24},{1,5},{5... | collective-permute-start | bytes 3317768 | tf_op jit(solution)/shard_map/ppermute | solution.py:239
  30.5 51.0 %collective-permute-start.1 = (bf16[2,432,640]{2,1,0:T(8,128)(2,1)S(1)}, bf16[2,432,640]{2,1,0:T(8,128)(2,1)S(1)}, u32[]{:S(2)}, u32[]{:S(2)}) collective-permute-start(bf16[2,432,640]{2,1,0:T(8,128)(2,1)S(1)} %copy-done.17), channel_id=1, source_target_pairs={{0,16},{4,20},{8,24},{12,28},{16,0},{20,4},{24,8},{28,12},{1,17},{... | collective-permute-start | bytes 3317768 | tf_op jit(solution)/shard_map/ppermute | solution.py:232
  81.5 25.7 %collective-permute-start.2 = (bf16[2,432,640]{2,1,0:T(8,128)(2,1)S(1)}, bf16[2,432,640]{2,1,0:T(8,128)(2,1)}, u32[]{:S(2)}, u32[]{:S(2)}) collective-permute-start(bf16[2,432,640]{2,1,0:T(8,128)(2,1)S(1)} %collective-permute-done.1.refs_3_), channel_id=1, source_target_pairs={{0,4},{4,0},{8,12},{12,8},{16,20},{20,16},{24,28},{28,24},{1,5},{5... | collective-permute-start | bytes 3317768 | tf_op jit(solution)/shard_map/ppermute | solution.py:239
  82.8 28.1 %collective-permute-start.3 = (bf16[2,432,640]{2,1,0:T(8,128)(2,1)}, bf16[2,432,640]{2,1,0:T(8,128)(2,1)}, u32[]{:S(2)}, u32[]{:S(2)}) collective-permute-start(bf16[2,432,640]{2,1,0:T(8,128)(2,1)} %pad_maximum_fusion.3), channel_id=1, source_target_pairs={{0,8},{4,12},{8,16},{12,20},{16,24},{20,28},{24,0},{28,4},{1,9},{5... | collective-permute-start | bytes 3317768 | tf_op jit(solution)/shard_map/ppermute | solution.py:232
  111.0 27.0 %collective-permute-start.5 = (bf16[2,432,640]{2,1,0:T(8,128)(2,1)}, bf16[2,432,640]{2,1,0:T(8,128)(2,1)}, u32[]{:S(2)}, u32[]{:S(2)}) collective-permute-start(bf16[2,432,640]{2,1,0:T(8,128)(2,1)} %pad_maximum_fusion.4), channel_id=1, source_target_pairs={{0,24},{4,28},{8,0},{12,4},{16,8},{20,12},{24,16},{28,20},{1,25},{... | collective-permute-start | bytes 3317768 | tf_op jit(solution)/shard_map/ppermute | solution.py:232
  119.5 47.0 %collective-permute-start.7 = (bf16[128,5120]{1,0:T(8,128)(2,1)}, bf16[128,5120]{1,0:T(8,128)(2,1)}, u32[]{:S(2)}, u32[]{:S(2)}) collective-permute-start(bf16[128,5120]{1,0:T(8,128)(2,1)} %multiply_convert_fusion.refs_9_), channel_id=1, source_target_pairs={{0,2},{1,3},{2,0},{3,1},{4,6},{5,7},{6,4},{7,5},{8,10},{9,11},{10,... | collective-permute-start | bytes 3932168 | tf_op jit(solution)/shard_map/ppermute | solution.py:247
  138.0 28.5 %collective-permute-start.10 = (bf16[128,5120]{1,0:T(8,128)(2,1)}, bf16[128,5120]{1,0:T(8,128)(2,1)}, u32[]{:S(2)}, u32[]{:S(2)}) collective-permute-start(bf16[128,5120]{1,0:T(8,128)(2,1)} %multiply_convert_fusion.refs_9_), channel_id=1, source_target_pairs={{0,8},{4,12},{8,16},{12,20},{16,24},{20,28},{1,9},{5,13},{9,17},{1... | collective-permute-start | bytes 3932168 | tf_op jit(solution)/shard_map/ppermute | solution.py:232
  141.1 30.2 %collective-permute-start.11 = (bf16[128,5120]{1,0:T(8,128)(2,1)}, bf16[128,5120]{1,0:T(8,128)(2,1)}, u32[]{:S(2)}, u32[]{:S(2)}) collective-permute-start(bf16[128,5120]{1,0:T(8,128)(2,1)} %multiply_convert_fusion.refs_9_), channel_id=1, source_target_pairs={{8,0},{12,4},{16,8},{20,12},{24,16},{28,20},{9,1},{13,5},{17,9},{2... | collective-permute-start | bytes 3932168 | tf_op jit(solution)/shard_map/ppermute | solution.py:232
  173.9 27.4 %collective-permute-start.12 = (bf16[128,5120]{1,0:T(8,128)(2,1)}, bf16[128,5120]{1,0:T(8,128)(2,1)}, u32[]{:S(2)}, u32[]{:S(2)}) collective-permute-start(bf16[128,5120]{1,0:T(8,128)(2,1)} %broadcast_select_fusion.1.refs_9_), channel_id=1, source_target_pairs={{0,2},{1,3},{2,0},{3,1},{4,6},{5,7},{6,4},{7,5},{8,10},{9,11},{10,... | collective-permute-start | bytes 3932168 | tf_op jit(solution)/shard_map/ppermute | solution.py:247
  175.5 25.9 %collective-permute-start.16 = (bf16[128,5120]{1,0:T(8,128)(2,1)}, bf16[128,5120]{1,0:T(8,128)(2,1)S(1)}, u32[]{:S(2)}, u32[]{:S(2)}) collective-permute-start(bf16[128,5120]{1,0:T(8,128)(2,1)} %collective-permute-done.10), channel_id=1, source_target_pairs={{8,16},{12,20},{16,24},{20,28},{9,17},{13,21},{17,25},{21,29},{10,... | collective-permute-start | bytes 3932168 | tf_op jit(solution)/shard_map/ppermute | solution.py:232
  176.2 30.8 %collective-permute-start.17 = (bf16[128,5120]{1,0:T(8,128)(2,1)}, bf16[128,5120]{1,0:T(8,128)(2,1)S(1)}, u32[]{:S(2)}, u32[]{:S(2)}) collective-permute-start(bf16[128,5120]{1,0:T(8,128)(2,1)} %collective-permute-done.11), channel_id=1, source_target_pairs={{8,0},{12,4},{16,8},{20,12},{9,1},{13,5},{17,9},{21,13},{10,2},{14... | collective-permute-start | bytes 3932168 | tf_op jit(solution)/shard_map/ppermute | solution.py:232
  231.4 28.9 %collective-permute-start.18 = (bf16[128,5120]{1,0:T(8,128)(2,1)}, bf16[128,5120]{1,0:T(8,128)(2,1)}, u32[]{:S(2)}, u32[]{:S(2)}) collective-permute-start(bf16[128,5120]{1,0:T(8,128)(2,1)} %broadcast_select_fusion.refs_9_), channel_id=1, source_target_pairs={{0,2},{1,3},{2,0},{3,1},{4,6},{5,7},{6,4},{7,5},{8,10},{9,11},{10,... | collective-permute-start | bytes 3932168 | tf_op jit(solution)/shard_map/ppermute | solution.py:247
  232.0 29.5 %collective-permute-start.8 = (bf16[128,5120]{1,0:T(8,128)(2,1)}, bf16[128,5120]{1,0:T(8,128)(2,1)S(1)}, u32[]{:S(2)}, u32[]{:S(2)}) collective-permute-start(bf16[128,5120]{1,0:T(8,128)(2,1)} %multiply_convert_fusion.refs_9_), channel_id=1, source_target_pairs={{0,1},{1,0},{2,3},{3,2},{4,5},{5,4},{6,7},{7,6},{8,9},{9,8},{10,11... | collective-permute-start | bytes 3932168 | tf_op jit(solution)/shard_map/ppermute | solution.py:256
  232.0 44.9 %collective-permute-start.9 = (bf16[128,5120]{1,0:T(8,128)(2,1)}, bf16[128,5120]{1,0:T(8,128)(2,1)}, u32[]{:S(2)}, u32[]{:S(2)}) collective-permute-start(bf16[128,5120]{1,0:T(8,128)(2,1)} %collective-permute-done.7.refs_10_), channel_id=1, source_target_pairs={{0,1},{1,0},{2,3},{3,2},{4,5},{5,4},{6,7},{7,6},{8,9},{9,8},{10,11... | collective-permute-start | bytes 3932168 | tf_op jit(solution)/shard_map/ppermute | solution.py:256
  260.9 27.2 %collective-permute-start.13 = (bf16[128,5120]{1,0:T(8,128)(2,1)}, bf16[128,5120]{1,0:T(8,128)(2,1)}, u32[]{:S(2)}, u32[]{:S(2)}) collective-permute-start(bf16[128,5120]{1,0:T(8,128)(2,1)} %broadcast_select_fusion.1.refs_9_), channel_id=1, source_target_pairs={{0,1},{1,0},{2,3},{3,2},{4,5},{5,4},{6,7},{7,6},{8,9},{9,8},{10,11... | collective-permute-start | bytes 3932168 | tf_op jit(solution)/shard_map/ppermute | solution.py:256
  260.9 27.2 %collective-permute-start.14 = (bf16[128,5120]{1,0:T(8,128)(2,1)}, bf16[128,5120]{1,0:T(8,128)(2,1)}, u32[]{:S(2)}, u32[]{:S(2)}) collective-permute-start(bf16[128,5120]{1,0:T(8,128)(2,1)} %collective-permute-done.12.refs_10_), channel_id=1, source_target_pairs={{0,1},{1,0},{2,3},{3,2},{4,5},{5,4},{6,7},{7,6},{8,9},{9,8},{10,11... | collective-permute-start | bytes 3932168 | tf_op jit(solution)/shard_map/ppermute | solution.py:256
  262.5 38.5 %collective-permute-start.19 = (bf16[128,5120]{1,0:T(8,128)(2,1)}, bf16[128,5120]{1,0:T(8,128)(2,1)}, u32[]{:S(2)}, u32[]{:S(2)}) collective-permute-start(bf16[128,5120]{1,0:T(8,128)(2,1)} %broadcast_select_fusion.refs_9_), channel_id=1, source_target_pairs={{0,1},{1,0},{2,3},{3,2},{4,5},{5,4},{6,7},{7,6},{8,9},{9,8},{10,11... | collective-permute-start | bytes 3932168 | tf_op jit(solution)/shard_map/ppermute | solution.py:256
  271.3 32.4 %collective-permute-start.20 = (bf16[128,5120]{1,0:T(8,128)(2,1)}, bf16[128,5120]{1,0:T(8,128)(2,1)}, u32[]{:S(2)}, u32[]{:S(2)}) collective-permute-start(bf16[128,5120]{1,0:T(8,128)(2,1)} %collective-permute-done.18.refs_10_), channel_id=1, source_target_pairs={{0,1},{1,0},{2,3},{3,2},{4,5},{5,4},{6,7},{7,6},{8,9},{9,8},{10,11... | collective-permute-start | bytes 3932168 | tf_op jit(solution)/shard_map/ppermute | solution.py:256
  271.3 45.5 %all-to-all-start.1 = ((bf16[8,128,512]{2,1,0:T(8,128)(2,1)}), bf16[8,128,512]{2,1,0:T(8,128)(2,1)}, u32[]{:S(2)}, u32[]{:S(2)}) async-start(bf16[8,128,512]{2,1,0:T(8,128)(2,1)} %bitcast.44), calls=%async_computation.1 | async-start | bytes 2097152 | tf_op jit(solution)/shard_map/all_to_all | solution.py:367
  276.9 26.8 %collective-permute-start.30 = (bf16[64,5120]{1,0:T(8,128)(2,1)}, bf16[64,5120]{1,0:T(8,128)(2,1)}, u32[]{:S(2)}, u32[]{:S(2)}) collective-permute-start(bf16[64,5120]{1,0:T(8,128)(2,1)} %get-tuple-element.41.refs_9_), channel_id=1, source_target_pairs={{0,2},{1,3},{2,0},{3,1},{4,6},{5,7},{6,4},{7,5},{8,10},{9,11},{10,... | collective-permute-start | bytes 1966088 | tf_op jit(solution)/shard_map/ppermute | solution.py:247
  303.6 26.4 %collective-permute-start.31 = (bf16[64,5120]{1,0:T(8,128)(2,1)}, bf16[64,5120]{1,0:T(8,128)(2,1)}, u32[]{:S(2)}, u32[]{:S(2)}) collective-permute-start(bf16[64,5120]{1,0:T(8,128)(2,1)} %get-tuple-element.41.refs_9_), channel_id=1, source_target_pairs={{0,1},{1,0},{2,3},{3,2},{4,5},{5,4},{6,7},{7,6},{8,9},{9,8},{10,11... | collective-permute-start | bytes 1966088 | tf_op jit(solution)/shard_map/ppermute | solution.py:256
  303.7 26.4 %collective-permute-start.32 = (bf16[64,5120]{1,0:T(8,128)(2,1)}, bf16[64,5120]{1,0:T(8,128)(2,1)}, u32[]{:S(2)}, u32[]{:S(2)}) collective-permute-start(bf16[64,5120]{1,0:T(8,128)(2,1)} %collective-permute-done.30.refs_10_), channel_id=1, source_target_pairs={{0,1},{1,0},{2,3},{3,2},{4,5},{5,4},{6,7},{7,6},{8,9},{9,8},{10,11... | collective-permute-start | bytes 1966088 | tf_op jit(solution)/shard_map/ppermute | solution.py:256
  314.7 32.1 %collective-permute-start.21 = (bf16[432,512]{1,0:T(8,128)(2,1)}, bf16[432,512]{1,0:T(8,128)(2,1)}, u32[]{:S(2)}, u32[]{:S(2)}) collective-permute-start(bf16[432,512]{1,0:T(8,128)(2,1)} %mlp_block.7), channel_id=1, source_target_pairs={{0,16},{4,20},{8,24},{12,28},{16,0},{20,4},{24,8},{28,12},{1,17},{... | collective-permute-start | bytes 1327112 | tf_op jit(solution)/shard_map/ppermute | solution.py:232
  (35 other events, 259.3 us)
